TPU v7x, 128 devices: a whole 4x4x4 slice. The times are simulated.
128 devices in a mesh: region: 16 (over x_lo, z, core), seq: 8 (over x_hi, y).
Axes of the slice: x: 4 (x_hi: 2, x_lo: 2; x = x_hi * 2 + x_lo), y: 4, z: 4, core: 2. Of those that a mesh axis runs over, the one named last changes fastest.
Arguments:
- tokens: bfloat16 [16384, 3584], P(('region', 'seq')), may hold values from -6 to 6
- preact: bfloat16 [16384, 10240], P('region', 'seq'), may hold values from -8 to 8
- cotangent: bfloat16 [16384, 10240], P('region', 'seq'), may hold values from -6 to 6
- master: float32 [3584, 10240], P('region', 'seq'), may hold values from -6 to 6
- first_moment: float32 [3584, 10240], P('region', 'seq'), may hold values from -1.5 to 1.5
- second_moment: float32 [3584, 10240], P('region', 'seq'), may hold values from 0.001 to 0.1
Outputs:
- new_master: float32 [3584, 10240], P('region', 'seq')
- new_first: float32 [3584, 10240], P('region', 'seq')
- new_second: float32 [3584, 10240], P('region', 'seq')
- input_grad: bfloat16 [16384, 3584], P(('region', 'seq'))
All inputs are finite; a program needn't handle non-finite values.
Results may differ from a plain program's by a relative error of at most 0.015.
Values may be sent and summed in bfloat16 or wider, within the bound.
A program may use at most 128 MiB of HBM per device.

v0:
```python
import jax
import jax.numpy as jnp
from jax import lax
from jax.sharding import PartitionSpec as P


def per_device(tokens, preact, cotangent, master, first_moment, second_moment):
    linear = preact.astype(jnp.float32)
    sigma = jax.nn.sigmoid(linear)
    slope = (cotangent.astype(jnp.float32) * sigma * (1.0 + linear * (1.0 - sigma))).astype(
        jnp.bfloat16
    )
    server_weights = master.astype(jnp.bfloat16)
    width = tokens.shape[1]
    scale = width ** (-0.5)
    owned_rows = master.shape[0]
    region_term = lax.dot_general(
        lax.all_gather(tokens, "seq", axis=0, tiled=True),
        slope,
        (((0,), (0,)), ((), ())),
        preferred_element_type=jnp.float32,
    )
    partial_sums = (
        lax.dot_general(
            slope,
            lax.all_gather(server_weights, "region", axis=0, tiled=True),
            (((1,), (1,)), ((), ())),
            preferred_element_type=jnp.float32,
        )
        * scale
    )
    gradient_in = lax.psum_scatter(
        partial_sums.astype(jnp.bfloat16), "seq", scatter_dimension=0, tiled=True
    )
    everything = lax.psum(region_term.astype(jnp.bfloat16), "region").astype(jnp.float32)
    offset = lax.axis_index("region") * owned_rows
    summed = lax.dynamic_slice_in_dim(everything, offset, owned_rows, 0)
    all_tokens = slope.shape[0] * lax.axis_size("region")
    pseudo = summed * all_tokens ** (-0.5)
    new_first = 0.9 * first_moment + 0.1 * pseudo
    new_second = 0.999 * second_moment + 0.001 * pseudo * pseudo
    new_master = master - 0.1 * new_first / (jnp.sqrt(new_second) + 0.001)
    return (new_master, new_first, new_second, gradient_in)


def solution(mesh):
    in_specs = (
        P(("region", "seq"), None),
        P("region", "seq"),
        P("region", "seq"),
        P("region", "seq"),
        P("region", "seq"),
        P("region", "seq"),
    )
    out_specs = (
        P("region", "seq"),
        P("region", "seq"),
        P("region", "seq"),
        P(("region", "seq"), None),
    )
    return jax.shard_map(
        per_device, mesh=mesh, in_specs=in_specs, out_specs=out_specs, check_vma=False
    )
```

profile of v0, /device:TPU:0, one launch (start us, length us, event | category | flops | bytes accessed | tf_op | source)
XLA Modules:
  0.0 433.7 jit_solution(10173714909304701077)
XLA Ops:
  7.2 0.0 copy-start.2
  7.2 0.0 all-gather.3.cloned.1.call-start
  7.2 0.7 all-gather.3.cloned.1.call-update
  7.9 0.0 all-gather.5.cloned.1.call-start
  8.0 2.1 convert_element_type.30
  10.1 0.0 all-gather.5.cloned.1.call-update
  10.1 0.0 all-reduce.2.cloned.1.call-start
  10.2 100.2 %all-gather.3.cloned.1.call-done = bf16[1024,3584]{1,0:T(8,128)(2,1)} async-done(((bf16[128,3584]{1,0:T(8,128)(2,1)}), bf16[1024,3584]{1,0:T(8,128)(2,1)}) %all-gather.3.cloned.1.call-update) | async-done | bytes 7340048 | tf_op jit(solution)/shard_map/all_gather | solution.py:18
  110.4 0.0 copy-done.2
  110.4 16.4 %fusion = bf16[3584,1280]{0,1:T(8,128)(2,1)} fusion(bf16[1024,3584]{1,0:T(8,128)(2,1)} %all-gather.3.cloned.1.call-done, bf16[1024,1280]{1,0:T(8,128)(2,1)S(1)} %copy-done.2, bf16[1024,1280]{1,0:T(8,128)(2,1)} %param.8), kind=kOutput, calls=%fused_computation.2 | convolution fusion | flops 9414246400 | bytes 21757952 | tf_op jit(solution)/shard_map/dot_general | solution.py:17
  126.7 0.0 all-reduce.2.cloned.1.call-update
  126.8 0.2 reduce-scatter.2.cloned.1.call-start
  127.0 39.5 %all-gather.5.cloned.1.call-done = bf16[3584,1280]{1,0:T(8,128)(2,1)} async-done(((bf16[224,1280]{1,0:T(8,128)(2,1)}), bf16[3584,1280]{1,0:T(8,128)(2,1)}) %all-gather.5.cloned.1.call-update) | async-done | bytes 9175056 | tf_op jit(solution)/shard_map/all_gather | solution.py:26
  166.5 17.9 %multiply_convert_fusion = bf16[1024,3584]{1,0:T(8,128)(2,1)} fusion(bf16[3584,1280]{1,0:T(8,128)(2,1)} %all-gather.5.cloned.1.call-done, bf16[1024,1280]{1,0:T(8,128)(2,1)S(1)} %copy-done.2, bf16[1024,1280]{1,0:T(8,128)(2,1)} %param.8), kind=kOutput, calls=%fused_computation.1 | convolution fusion | flops 9416998912 | bytes 21757952 | tf_op jit(solution)/shard_map/dot_general | solution.py:24
  184.3 0.0 copy-start.1
  184.3 0.0 reduce-scatter.2.cloned.1.call-update
  184.4 1.3 copy-done.1
  185.6 0.4 copy.12
  186.0 1.7 copy.10
  187.7 2.7 copy.11
  190.5 125.0 %all-reduce.2.cloned.1.call-done = bf16[3584,1280]{0,1:T(8,128)(2,1)} async-done(((bf16[3584,1280]{0,1:T(8,128)(2,1)}), bf16[3584,1280]{0,1:T(8,128)(2,1)}) %all-reduce.2.cloned.1.call-update) | async-done | bytes 9175056 | tf_op jit(solution)/shard_map/psum | solution.py:35
  315.5 4.5 %divide_subtract_fusion = (f32[224,1280]{0,1:T(8,128)}, f32[224,1280]{0,1:T(8,128)}, f32[224,1280]{0,1:T(8,128)}) fusion(f32[224,1280]{0,1:T(8,128)S(1)} %copy.12, bf16[3584,1280]{0,1:T(8,128)(2,1)} %all-reduce.2.cloned.1.call-done, s32[]{:T(128)S(6)} %select_n.3, f32[224,1280]{0,1:T(8,128)S(1)} %copy.10, f32[224,1280]{0,1:T(8,128)} %copy.11), kind=kLoop, calls=%fused_computation.17 | loop fusion | flops 3727360 | bytes 7454724 | tf_op jit(solution)/shard_map/sub | solution.py:42
  320.0 0.0 copy-start
  320.0 2.8 copy.13
  322.8 2.7 copy.14
  325.5 0.0 copy-done
  325.5 1.4 copy.15
  326.9 100.2 %reduce-scatter.2.cloned.1.call-done = bf16[128,3584]{1,0:T(8,128)(2,1)} async-done(((bf16[1024,3584]{1,0:T(8,128)(2,1)}), bf16[128,3584]{1,0:T(8,128)(2,1)}) %reduce-scatter.2.cloned.1.call-update) | async-done | bytes 917520 | tf_op jit(solution)/shard_map/reduce_scatter | solution.py:32
Async XLA Ops:
  7.2 103.2 %copy-start.2 = (bf16[1024,1280]{1,0:T(8,128)(2,1)S(1)}, bf16[1024,1280]{1,0:T(8,128)(2,1)}, u32[]{:S(2)}) copy-start(bf16[1024,1280]{1,0:T(8,128)(2,1)} %param.7) | copy-start | bytes 7864324
  7.2 103.2 %all-gather.3.cloned.1.call-start = ((), (), s32[]{:S(2)}) async-start(), calls=%async_computation.1 | async-start | bytes 8257536 | tf_op jit(solution)/shard_map/all_gather | solution.py:18
  7.9 158.6 %all-gather.5.cloned.1.call-start = ((), (), s32[]{:S(2)}) async-start(), calls=%async_computation.3 | async-start | bytes 9748480 | tf_op jit(solution)/shard_map/all_gather | solution.py:26
  10.1 305.4 %all-reduce.2.cloned.1.call-start = ((), (), s32[]{:S(2)}) async-start(), calls=%async_computation.2 | async-start | bytes 18350080 | tf_op jit(solution)/shard_map/psum | solution.py:35
  126.8 300.4 %reduce-scatter.2.cloned.1.call-start = ((), (), s32[]{:S(2)}) async-start(), calls=%async_computation.4 | async-start | bytes 8257536 | tf_op jit(solution)/shard_map/reduce_scatter | solution.py:32
  184.3 1.3 copy-start.1
  320.0 5.5 %copy-start = (f32[224,1280]{0,1:T(8,128)S(1)}, f32[224,1280]{0,1:T(8,128)}, u32[]{:S(2)}) copy-start(f32[224,1280]{0,1:T(8,128)} %get-tuple-element.10) | copy-start | bytes 3440644
Sparse Core Ops, SparseCore 0:
  10.3 100.0 all-gather.2
  112.7 53.7 all-gather.4
  169.0 146.4 all-reduce.1
  320.3 106.8 reduce-scatter.1
where the time goes:
time: 434 us
  waiting for transfers between devices  366 us (84%)
  matrix products  34.2 us (8%)
  between operations  13.8 us (3%)
  local copies, waits for them, and re-layouts  13 us (3%)
  other arithmetic  6.64 us (2%)
    psum x1, waiting for transfers between devices, per_device(): lax.psum(region_term.astype(jnp.bfloat16), 'region').astype(jnp.float32)  125 us
    reduce_scatter x1, waiting for transfers between devices, per_device(): lax.psum_scatter(partial_sums.astype(jnp.bfloat16), 'seq', scatter_dimens...  100 us
    all_gather x1, waiting for transfers between devices, per_device(): lax.all_gather(tokens, 'seq', axis=0, tiled=True)  100 us
    all_gather x1, waiting for transfers between devices, per_device(): lax.all_gather(server_weights, 'region', axis=0, tiled=True)  39.5 us
    dot_general x1, matrix products, per_device(): lax.dot_general(slope, lax.all_gather(server_weights, 'region', axis=0, t...  17.9 us
    dot_general x1, matrix products, per_device(): lax.dot_general(lax.all_gather(tokens, 'seq', axis=0, tiled=True), slope,...  16.4 us
    unnamed x12, local copies, waits for them, and re-layouts  13 us
  transfers between devices with their start and end apart: 4, of which 4 were waited for; matrix products, arithmetic and copies ran while one was open for 12% of the time, Pallas kernels for 0%

commit v1 on v0

v1 whole, which is shorter than its diff:
```python
import jax
import jax.numpy as jnp
from jax import lax
from jax.experimental import pallas as pl
from jax.experimental.pallas import tpu as pltpu
from jax.sharding import PartitionSpec as P

MESH = pl.DeviceIdType.MESH
BF = jnp.bfloat16
F32 = jnp.float32

D = 3584
REGIONS = 16
SEQS = 8
OWN = D // REGIONS
CH = 7
RB = OWN // CH
CD = D // CH
TOK = 128
HID = 1280
RT = TOK * SEQS
STAGE = 128


def place(d0):
    owner, rest = divmod(d0, OWN)
    k, i = divmod(rest, RB)
    xl, z, c = owner // 8, owner // 2 % 4, owner % 2
    return k, ((c * 2 + xl) * 4 + z) * RB + i


def rcopy(src, dst, send, recv, dev):
    return pltpu.make_async_remote_copy(
        src_ref=src, dst_ref=dst, send_sem=send, recv_sem=recv, device_id=dev, device_id_type=MESH
    )


def kernel(
    tok, pre, cot, mas, sum_out, ig_out,
    tg, wg, slope, tb, cr, zf, zn, xlb, ib, yf, yn, xhb, tokv, masv, prev, cotv,
    in_sem, st_sem, ts, tr, ws, wr, us, ur, vs, vr,
):
    r = lax.axis_index("region")
    s = lax.axis_index("seq")
    xl, z, c = r // 8, (r // 2) % 4, r % 2
    xh, y = s // 4, s % 4
    ol, oh = 1 - xl, 1 - xh
    zp, zm, zo = (z + 1) % 4, (z + 3) % 4, (z + 2) % 4
    yp, ym, yo = (y + 1) % 4, (y + 3) % 4, (y + 2) % 4

    def rdev(a, b, d):
        return (a * 8 + b * 2 + d, s)

    def sdev(a, b):
        return (r, a * 4 + b)

    d_core = rdev(xl, z, 1 - c)
    d_xl = rdev(ol, z, c)
    d_zp = rdev(xl, zp, c)
    d_zm = rdev(xl, zm, c)
    d_xh = sdev(oh, y)
    d_yp = sdev(xh, yp)
    d_ym = sdev(xh, ym)

    get_tok = pltpu.make_async_copy(tok, tokv, in_sem.at[0])
    get_mas = pltpu.make_async_copy(mas, masv, in_sem.at[1])
    get_tok.start()
    get_mas.start()

    def stage(i, slot):
        rows = pl.ds(pl.multiple_of(i * STAGE, STAGE), STAGE)
        return (
            pltpu.make_async_copy(pre.at[rows], prev.at[slot], st_sem.at[0, slot]),
            pltpu.make_async_copy(cot.at[rows], cotv.at[slot], st_sem.at[1, slot]),
        )

    for i in range(2):
        for copy in stage(i, i):
            copy.start()

    barrier = pltpu.get_barrier_semaphore()
    for dev in (d_core, d_xl, d_zp, d_zm, d_xh, d_yp, d_ym):
        pl.semaphore_signal(barrier, inc=1, device_id=dev, device_id_type=MESH)

    get_tok.wait()
    for j in range(D // 128):
        turned = tokv[:, j * 128:(j + 1) * 128].T
        for m in range(128 // RB):
            k, row = place(j * 128 + m * RB)
            tg[k, s, row:row + RB, :] = turned[m * RB:(m + 1) * RB, :]
    get_mas.wait()
    w_own = xl * 4 + z
    w_oth = ol * 4 + z

    def cast(k, carry):
        wg[k, c, w_own] = masv[k].astype(BF)
        return carry

    lax.fori_loop(0, CH, cast, 0)
    pl.semaphore_wait(barrier, 7)

    def t_copy(k, slot, i, j, dev):
        return rcopy(tg.at[k, slot], tg.at[k, slot], ts.at[k, i], tr.at[k, j], dev)

    def w_copy(k, slot, i, j, dev):
        return rcopy(wg.at[k, c, slot], wg.at[k, c, slot], ws.at[k, i], wr.at[k, j], dev)

    def w_core(k):
        return rcopy(wg.at[k, c], wg.at[k, c], ws.at[k, 7], wr.at[k, 7], d_core)

    def gather0(k, carry):
        t_copy(k, s, 0, 0, d_xh).start()
        t_copy(k, s, 1, 1 + xh, d_yp).start()
        t_copy(k, s, 2, 3 + xh, d_ym).start()
        w_copy(k, w_own, 0, 0, d_xl).start()
        w_copy(k, w_own, 1, 1 + xl, d_zp).start()
        w_copy(k, w_own, 2, 3 + xl, d_zm).start()
        return carry

    def t_wait(k, slot, j):
        t_copy(k, slot, 0, j, d_xh).wait_recv()

    def w_wait(k, slot, j):
        w_copy(k, slot, 0, j, d_xl).wait_recv()

    def gather1(k):
        t_wait(k, oh * 4 + y, 0)
        t_copy(k, oh * 4 + y, 3, 1 + oh, d_yp).start()
        t_copy(k, oh * 4 + y, 4, 3 + oh, d_ym).start()
        w_wait(k, w_oth, 0)
        w_copy(k, w_oth, 3, 1 + ol, d_zp).start()
        w_copy(k, w_oth, 4, 3 + ol, d_zm).start()

    def gather2(k):
        t_wait(k, ym, 1)
        t_copy(k, ym, 5, 5, d_yp).start()
        t_wait(k, 4 + yp, 4)
        t_copy(k, 4 + yp, 6, 6, d_ym).start()
        w_wait(k, zm, 1)
        w_copy(k, zm, 5, 5, d_zp).start()
        w_wait(k, 4 + zp, 4)
        w_copy(k, 4 + zp, 6, 6, d_zm).start()

    def gather3(k):
        w_wait(k, 4 + zm, 2)
        w_wait(k, zp, 3)
        w_wait(k, zo, 5)
        w_wait(k, 4 + zo, 6)
        w_core(k).start()
        t_wait(k, 4 + ym, 2)
        t_wait(k, yp, 3)
        t_wait(k, yo, 5)
        t_wait(k, 4 + yo, 6)

    def u_core(k):
        return rcopy(tb.at[k, 1 - c], cr.at[k], us.at[k, 0], ur.at[k, 0], d_core)

    def u_far(k, p):
        slot = (zo, 4 + zo)[p]
        return rcopy(tb.at[k, c, slot], zf.at[k, p], us.at[k, 1 + p], ur.at[k, 1 + p], (d_zp, d_zm)[p])

    def u_near(k, p, a):
        slot = (zp, zm)[p] + 4 * a
        i = 3 + 2 * p + a
        return rcopy(tb.at[k, c, slot], zn.at[k, p, a], us.at[k, i], ur.at[k, i], (d_zp, d_zm)[p])

    def u_last(k):
        return rcopy(tb.at[k, c, w_oth], xlb.at[k], us.at[k, 7], ur.at[k, 7], d_xl)

    def v_far(k, p):
        slot = (yo, 4 + yo)[p]
        return rcopy(ib.at[k, slot], yf.at[k, p], vs.at[k, 1 + p], vr.at[k, 1 + p], (d_yp, d_ym)[p])

    def v_near(k, p, a):
        slot = (yp, ym)[p] + 4 * a
        i = 3 + 2 * p + a
        return rcopy(ib.at[k, slot], yn.at[k, p, a], vs.at[k, i], vr.at[k, i], (d_yp, d_ym)[p])

    def v_last(k):
        return rcopy(ib.at[k, oh * 4 + y], xhb.at[k], vs.at[k, 7], vr.at[k, 7], d_xh)

    def multiply(k):
        def term(j, carry):
            cols = pl.ds(pl.multiple_of(j * 256, 256), 256)
            left = jnp.concatenate([tg[k, i] for i in range(SEQS)], axis=1)
            out = jnp.dot(left, slope[:, cols], preferred_element_type=F32)
            tb[k, :, :, :, cols] = out.astype(BF).reshape(2, 8, RB, 256)
            return carry

        lax.fori_loop(0, HID // 256, term, 0)
        u_core(k).start()
        rcopy(wg.at[k, 1 - c], wg.at[k, 1 - c], ws.at[k, 7], wr.at[k, 7], d_core).wait_recv()

        def part(j, carry):
            rows = pl.ds(pl.multiple_of(j * 256, 256), 256)
            left = wg[k].reshape(CD, HID)
            out = lax.dot_general(
                left, slope[rows, :], (((1,), (1,)), ((), ())), preferred_element_type=F32
            )
            out = (out * D ** (-0.5)).astype(BF)
            ib[k, 2 * j] = out[:, :128]
            ib[k, 2 * j + 1] = out[:, 128:]
            return carry

        lax.fori_loop(0, RT // 256, part, 0)
        v_far(k, 0).start()
        v_far(k, 1).start()
        v_near(k, 0, 1).start()
        v_near(k, 1, 0).start()
        u_core(k).wait_recv()

        def add(i, carry):
            tb[k, c, i] = (tb[k, c, i].astype(F32) + cr[k, i].astype(F32)).astype(BF)
            return carry

        lax.fori_loop(0, 8, add, 0)
        u_far(k, 0).start()
        u_far(k, 1).start()
        u_near(k, 0, 1).start()
        u_near(k, 1, 0).start()

    def scatter2(k):
        for p in range(2):
            slot = (yp, ym)[p] + 4 * p
            v_far(k, p).wait_recv()
            ib[k, slot] = (ib[k, slot].astype(F32) + yf[k, p].astype(F32)).astype(BF)
            v_near(k, p, p).start()
        for p in range(2):
            slot = (zp, zm)[p] + 4 * p
            u_far(k, p).wait_recv()
            tb[k, c, slot] = (tb[k, c, slot].astype(F32) + zf[k, p].astype(F32)).astype(BF)
            u_near(k, p, p).start()

    def scatter3(k):
        for p in range(2):
            for a in range(2):
                v_near(k, p, a).wait_recv()
        slot = oh * 4 + y
        ib[k, slot] = (
            ib[k, slot].astype(F32) + yn[k, 0, oh].astype(F32) + yn[k, 1, oh].astype(F32)
        ).astype(BF)
        v_last(k).start()
        for p in range(2):
            for a in range(2):
                u_near(k, p, a).wait_recv()
        tb[k, c, w_oth] = (
            tb[k, c, w_oth].astype(F32) + zn[k, 0, ol].astype(F32) + zn[k, 1, ol].astype(F32)
        ).astype(BF)
        u_last(k).start()

    def scatter4(k):
        v_last(k).wait_recv()
        ig_out[k] = (
            (ib[k, s].astype(F32) + xhb[k].astype(F32))
            + (yn[k, 0, xh].astype(F32) + yn[k, 1, xh].astype(F32))
        ).astype(BF)
        u_last(k).wait_recv()
        sum_out[k] = (tb[k, c, w_own].astype(F32) + xlb[k].astype(F32)) + (
            zn[k, 0, xl].astype(F32) + zn[k, 1, xl].astype(F32)
        )

    lax.fori_loop(0, CH, gather0, 0)

    def make_slope(i, carry):
        slot = i % 2
        for copy in stage(i, slot):
            copy.wait()
        lin = prev[slot].astype(F32)
        sig = jax.nn.sigmoid(lin)
        rows = pl.ds(pl.multiple_of(i * STAGE, STAGE), STAGE)
        slope[rows, :] = (cotv[slot].astype(F32) * sig * (1.0 + lin * (1.0 - sig))).astype(BF)

        @pl.when(i + 2 < RT // STAGE)
        def _():
            for copy in stage(i + 2, slot):
                copy.start()

        return carry

    lax.fori_loop(0, RT // STAGE, make_slope, 0)

    def step(t, carry):
        def at(lag, work):
            k = t - lag

            @pl.when((k >= 0) & (k < CH))
            def _():
                work(k)

        at(0, gather1)
        at(1, gather2)
        at(2, gather3)
        at(2, multiply)
        at(3, scatter2)
        at(4, scatter3)
        at(5, scatter4)
        return carry

    lax.fori_loop(0, CH + 5, step, 0)

    def drain(k, carry):
        for i in range(7):
            t_copy(k, s, i, 0, d_xh).wait_send()
            w_copy(k, w_own, i, 0, d_xl).wait_send()
        w_core(k).wait_send()
        u_core(k).wait_send()
        u_last(k).wait_send()
        v_last(k).wait_send()
        for p in range(2):
            u_far(k, p).wait_send()
            v_far(k, p).wait_send()
            for a in range(2):
                u_near(k, p, a).wait_send()
                v_near(k, p, a).wait_send()
        return carry

    lax.fori_loop(0, CH, drain, 0)


def exchange(tokens, preact, cotangent, master):
    any_spec = pl.BlockSpec(memory_space=pl.ANY)
    vmem = pl.BlockSpec(memory_space=pltpu.VMEM)
    dma = pltpu.SemaphoreType.DMA
    return pl.pallas_call(
        kernel,
        out_shape=(
            jax.ShapeDtypeStruct((CH, RB, HID), F32),
            jax.ShapeDtypeStruct((CH, CD, TOK), BF),
        ),
        in_specs=[any_spec] * 4,
        out_specs=(vmem, vmem),
        scratch_shapes=[
            pltpu.VMEM((CH, SEQS, CD, TOK), BF),
            pltpu.VMEM((CH, 2, 8, RB, HID), BF),
            pltpu.VMEM((RT, HID), BF),
            pltpu.VMEM((CH, 2, 8, RB, HID), BF),
            pltpu.VMEM((CH, 8, RB, HID), BF),
            pltpu.VMEM((CH, 2, RB, HID), BF),
            pltpu.VMEM((CH, 2, 2, RB, HID), BF),
            pltpu.VMEM((CH, RB, HID), BF),
            pltpu.VMEM((CH, SEQS, CD, TOK), BF),
            pltpu.VMEM((CH, 2, CD, TOK), BF),
            pltpu.VMEM((CH, 2, 2, CD, TOK), BF),
            pltpu.VMEM((CH, CD, TOK), BF),
            pltpu.VMEM((TOK, D), BF),
            pltpu.VMEM((CH, RB, HID), F32),
            pltpu.VMEM((2, STAGE, HID), BF),
            pltpu.VMEM((2, STAGE, HID), BF),
            dma((2,)),
            dma((2, 2)),
            dma((CH, 8)),
            dma((CH, 8)),
            dma((CH, 8)),
            dma((CH, 8)),
            dma((CH, 8)),
            dma((CH, 8)),
            dma((CH, 8)),
            dma((CH, 8)),
        ],
        compiler_params=pltpu.CompilerParams(
            collective_id=0, has_side_effects=True, vmem_limit_bytes=62 * 2**20
        ),
        cost_estimate=pl.CostEstimate(
            flops=4 * RT * HID * D, bytes_accessed=12 * 2**20, transcendentals=RT * HID
        ),
        name="exchange",
    )(tokens, preact, cotangent, master)


def per_device(tokens, preact, cotangent, master, first_moment, second_moment):
    summed, turned = exchange(tokens, preact, cotangent, master.reshape(CH, RB, HID))
    turned = turned.reshape(CH, 2, 2, 4, RB, TOK)
    input_grad = turned.transpose(5, 2, 3, 1, 0, 4).reshape(TOK, D)
    pseudo = summed.reshape(OWN, HID) * (RT * REGIONS) ** (-0.5)
    new_first = 0.9 * first_moment + 0.1 * pseudo
    new_second = 0.999 * second_moment + 0.001 * pseudo * pseudo
    new_master = master - 0.1 * new_first / (jnp.sqrt(new_second) + 0.001)
    return (new_master, new_first, new_second, input_grad)


def solution(mesh):
    block = P("region", "seq")
    rows = P(("region", "seq"), None)
    return jax.shard_map(
        per_device,
        mesh=mesh,
        in_specs=(rows, block, block, block, block, block),
        out_specs=(block, block, block, rows),
        check_vma=False,
    )
```

time: 434 us -> 148 us (0.34)
  waiting for transfers between devices: 366 us -> 0 us
  Pallas kernels: 0 us -> 141 us
  matrix products: 34.2 us -> 0 us
  between operations: 13.8 us -> 0.67 us
  local copies, waits for them, and re-layouts: 13 us -> 4.28 us
  other arithmetic: 6.64 us -> 2.3 us
    pallas_call x0 -> x1, Pallas kernels: none -> 141 us  [exchange(): pl.pallas_call(kernel, out_shape=(jax.ShapeDtypeStruct((CH, RB, HID), F32...]
    all_gather x2 -> x0, waiting for transfers between devices: 140 us -> none  [the longest x1 100 us: per_device(): lax.all_gather(tokens, 'seq', axis=0, tiled=True)]
    psum x1 -> x0, waiting for transfers between devices: 125 us -> none  [per_device(): lax.psum(region_term.astype(jnp.bfloat16), 'region').astype(jnp.float32)]
    reduce_scatter x1 -> x0, waiting for transfers between devices: 100 us -> none  [per_device(): lax.psum_scatter(partial_sums.astype(jnp.bfloat16), 'seq', scatter_dimens...]
    dot_general x2 -> x0, matrix products: 34.2 us -> none  [the longest x1 17.9 us: per_device(): lax.dot_general(slope, lax.all_gather(server_weights, 'region', axis=0, t...]
    unnamed x12 -> x9, local copies, waits for them, and re-layouts: 13 us -> 3.02 us
  transfers between devices with their start and end apart: 4 -> 0, of which waited for: 4 -> 0; matrix products, arithmetic and copies ran while one was open for 12% -> 0% of each run, Pallas kernels for 0% -> 0%
where the time goes in v1:
time: 148 us
  Pallas kernels  141 us (95%)
  local copies, waits for them, and re-layouts  4.28 us (3%)
  other arithmetic  2.3 us (2%)
    pallas_call x1, Pallas kernels, exchange(): pl.pallas_call(kernel, out_shape=(jax.ShapeDtypeStruct((CH, RB, HID), F32...  141 us
    unnamed x9, local copies, waits for them, and re-layouts  3.02 us

profile of v1, /device:TPU:0, one launch (start us, length us, event | category | flops | bytes accessed | tf_op | source)
XLA Modules:
  0.0 148.2 jit_solution(2794880402963517818)
XLA Ops:
  0.6 141.0 %exchange.1 = (f32[7,32,1280]{2,1,0:T(8,128)}, bf16[7,512,128]{2,1,0:T(8,128)(2,1)}) custom-call(bf16[128,3584]{1,0:T(8,128)(2,1)} %tok.1, bf16[1024,1280]{1,0:T(8,128)(2,1)} %pre.1, bf16[1024,1280]{1,0:T(8,128)(2,1)} %cot.1, f32[7,32,1280]{2,1,0:T(8,128)} %bitcast.12), custom_call_target="tpu_custom_call" | custom-call | flops 18790481920 | bytes 12582912 | tf_op jit(solution)/shard_map/exchange/pallas_call | solution.py:324
  141.6 1.3 copy.11
  142.9 0.0 copy-start.3
  142.9 1.3 copy.12
  144.2 0.0 copy-done.3
  144.2 0.0 copy-start
  144.2 0.0 copy-start.1
  144.2 0.0 copy-start.2
  144.2 0.2 multiply_multiply_fusion
  144.5 1.0 copy-done
  145.5 0.3 copy-done.1
  145.8 0.3 copy-done.2
  146.2 2.0 %divide_subtract_fusion = (f32[224,1280]{1,0:T(8,128)}, f32[224,1280]{1,0:T(8,128)}, f32[224,1280]{1,0:T(8,128)}) fusion(f32[224,1280]{1,0:T(8,128)S(1)} %copy-done, f32[7,32,1280]{2,1,0:T(8,128)S(1)} %get-tuple-element.16, f32[224,1280]{1,0:T(8,128)S(1)} %copy-done.1, f32[7,32,1280]{2,1,0:T(8,128)S(1)} %get-tuple-element.15, f32[224,1280]{1,0:T(8,128)S(1)} %copy-done.2), kind=kLoop, calls=%fused_computation.2 | loop fusion | flops 2293760 | bytes 9175040 | tf_op jit(solution)/shard_map/sub | solution.py:377
Async XLA Ops:
  142.9 1.3 copy-start.3
  144.2 1.3 copy-start
  144.2 1.6 %copy-start.1 = (f32[224,1280]{1,0:T(8,128)S(1)}, f32[224,1280]{1,0:T(8,128)}, u32[]{:S(2)}) copy-start(f32[224,1280]{1,0:T(8,128)} %param.10) | copy-start | bytes 3440644
  144.2 1.9 %copy-start.2 = (f32[224,1280]{1,0:T(8,128)S(1)}, f32[224,1280]{1,0:T(8,128)}, u32[]{:S(2)}) copy-start(f32[224,1280]{1,0:T(8,128)} %param.11) | copy-start | bytes 3440644

commit v2 on v1

v2 whole, which is shorter than its diff:
```python
import jax
import jax.numpy as jnp
from jax import lax
from jax.experimental import pallas as pl
from jax.experimental.pallas import tpu as pltpu
from jax.sharding import PartitionSpec as P

MESH = pl.DeviceIdType.MESH
BF = jnp.bfloat16
F32 = jnp.float32

D = 3584
REGIONS = 16
SEQS = 8
OWN = D // REGIONS
CH = 7
RB = OWN // CH
CD = D // CH
HALF = CD // 2
TOK = 128
HID = 1280
RT = TOK * SEQS
STAGE = 128
Y_FIRST = (2, 4)

ORDER = (
    ("t_own", 1), ("w_own", 1), ("t_cross", 0), ("t_own", 2), ("w_own", 0), ("t_own", 3), ("t_own", 0),
    ("w_own", 5), ("t_cross", 6), ("w_other", 1), ("slope", -1), ("w_own", 2), ("w_own", 3), ("w_pass1", 1),
    ("t_cross", 1), ("t_own", 4), ("w_pass0", 1), ("w_own", 6), ("t_cross", 3), ("t_other", 0),
    ("w_other", 2), ("w_pass0", 3), ("w_pass0", 5), ("w_pass0", 0), ("t_pass0", 0), ("t_own", 5),
    ("w_other", 0), ("t_pass0", 1), ("t_pass1", 0), ("w_other", 5), ("t_other", 1), ("w_own", 4),
    ("w_pass1", 0), ("t_pass0", 2), ("t_other", 6), ("t_pass1", 4), ("t_other", 3), ("w_other", 3),
    ("t_pass1", 1), ("w_pass1", 3), ("w_other", 6), ("t_pass1", 2), ("t_cross", 5), ("w_pass0", 6),
    ("w_other", 4), ("t_pass0", 4), ("w_share", 1), ("w_pass1", 5), ("term", 0), ("w_pass1", 6),
    ("w_pass0", 4), ("w_share", 3), ("w_pass1", 2), ("t_own", 6), ("part", 1), ("w_pass1", 4),
    ("t_pass0", 3), ("t_other", 5), ("t_far", 4), ("w_pass0", 2), ("term", 1), ("u_first", 0),
    ("w_share", 6), ("t_far", 2), ("w_share", 4), ("t_pass1", 3), ("t_cross", 4), ("w_share", 2),
    ("part", 3), ("u_first", 1), ("u_pass0", 0), ("t_cross", 2), ("t_pass1", 6), ("u_pass0", 1),
    ("part", 2), ("w_share", 0), ("t_pass0", 5), ("term", 4), ("term", 2), ("u_pass1", 1), ("t_pass1", 5),
    ("w_share", 5), ("u_first", 4), ("t_pass0", 6), ("v_pass0", 3), ("v_pass0", 1), ("part", 0),
    ("u_cross", 1), ("part", 4), ("term", 5), ("u_first", 2), ("v_pass1", 1), ("term", 3), ("v_pass1", 3),
    ("u_first", 5), ("v_pass1", 0), ("v_cross", 1), ("u_pass0", 4), ("u_pass0", 2), ("v_pass0", 0),
    ("part", 5), ("u_first", 3), ("part", 6), ("u_cross", 4), ("term", 6), ("u_pass1", 2), ("u_pass1", 4),
    ("v_cross", 0), ("v_pass0", 5), ("u_pass0", 3), ("v_end", 1), ("u_cross", 0), ("u_first", 6),
    ("v_cross", 3), ("v_end", 0), ("u_pass1", 5), ("u_pass0", 5), ("v_pass0", 6), ("u_cross", 2),
    ("u_cross", 3), ("v_first", 4), ("u_pass1", 0), ("v_pass1", 6), ("v_first", 2), ("v_cross", 5),
    ("u_end", 0), ("u_pass0", 6), ("u_cross", 5), ("v_end", 3), ("v_pass1", 5), ("u_pass1", 3),
    ("v_cross", 4), ("v_cross", 6), ("u_cross", 6), ("v_cross", 2), ("u_pass1", 6), ("u_end", 2),
    ("u_end", 3), ("v_end", 6), ("v_end", 4), ("u_end", 5), ("u_end", 1), ("v_end", 5), ("u_end", 4),
    ("u_end", 6), ("v_end", 2),
)


def place(d0):
    owner, rest = divmod(d0, OWN)
    k, i = divmod(rest, RB)
    xl, z, c = owner // 8, owner // 2 % 4, owner % 2
    return k, ((c * 2 + xl) * 4 + z) * RB + i


def rcopy(src, dst, send, recv, dev):
    return pltpu.make_async_remote_copy(
        src_ref=src, dst_ref=dst, send_sem=send, recv_sem=recv, device_id=dev, device_id_type=MESH
    )


def plus(*refs):
    total = refs[0][...].astype(F32)
    for ref in refs[1:]:
        total = total + ref[...].astype(F32)
    return total


def kernel(
    tok, pre, cot, mas, sum_out, ig_out,
    tg, wg, slope, tb, cr, zf, zn, xlb, ib, yf, yn, xhb, tokv, masv, prev, cotv,
    in_sem, st_sem, ts, tr, ws, wr, us, ur, vs, vr,
):
    r = lax.axis_index("region")
    s = lax.axis_index("seq")
    xl, z, c = r // 8, (r // 2) % 4, r % 2
    xh, y = s // 4, s % 4
    ol, oh = 1 - xl, 1 - xh
    zp, zm, zo = (z + 1) % 4, (z + 3) % 4, (z + 2) % 4
    yp, ym, yo = (y + 1) % 4, (y + 3) % 4, (y + 2) % 4

    def rdev(a, b, d):
        return (a * 8 + b * 2 + d, s)

    def sdev(a, b):
        return (r, a * 4 + b)

    d_core = rdev(xl, z, 1 - c)
    d_xl = rdev(ol, z, c)
    d_z = (rdev(xl, zp, c), rdev(xl, zm, c))
    d_xh = sdev(oh, y)
    d_y = (sdev(xh, yp), sdev(xh, ym))

    get_tok = pltpu.make_async_copy(tok, tokv, in_sem.at[0])
    get_mas = pltpu.make_async_copy(mas, masv, in_sem.at[1])
    get_tok.start()
    get_mas.start()

    def stage(i, slot):
        rows = pl.ds(pl.multiple_of(i * STAGE, STAGE), STAGE)
        return (
            pltpu.make_async_copy(pre.at[rows], prev.at[slot], st_sem.at[0, slot]),
            pltpu.make_async_copy(cot.at[rows], cotv.at[slot], st_sem.at[1, slot]),
        )

    for i in range(2):
        for copy in stage(i, i):
            copy.start()

    barrier = pltpu.get_barrier_semaphore()
    for dev in (d_core, d_xl, *d_z, d_xh, *d_y):
        pl.semaphore_signal(barrier, inc=1, device_id=dev, device_id_type=MESH)

    get_tok.wait()
    for j in range(D // 128):
        turned = tokv[:, j * 128:(j + 1) * 128].T
        for m in range(128 // RB):
            k, row = place(j * 128 + m * RB)
            tg[k, s, row:row + RB, :] = turned[m * RB:(m + 1) * RB, :]
    get_mas.wait()

    def cast(k, carry):
        wg[k, c, xl * 4 + z] = masv[k].astype(BF)
        return carry

    lax.fori_loop(0, CH, cast, 0)
    pl.semaphore_wait(barrier, 7)

    def t_copy(k, slot, i, dev):
        return rcopy(tg.at[k, slot], tg.at[k, slot], ts.at[k, i], tr.at[k, i], dev)

    def t_half(k, slot, p):
        part = tg.at[k, slot, pl.ds(p * HALF, HALF)]
        return rcopy(part, part, ts.at[k, 5 + p], tr.at[k, 5 + p], d_y[p])

    def t_wait(k, *ids):
        for i in ids:
            t_copy(k, 0, i, d_xh).wait_recv()

    def t_cross(k):
        t_copy(k, s, 0, d_xh).start()

    def t_own(k):
        t_copy(k, s, 1, d_y[0]).start()
        t_copy(k, s, 3, d_y[1]).start()

    def t_other(k):
        t_wait(k, 0)
        t_copy(k, oh * 4 + y, 2, d_y[0]).start()
        t_copy(k, oh * 4 + y, 4, d_y[1]).start()

    def t_pass0(k):
        t_wait(k, 1)
        if k in Y_FIRST:
            t_half(k, xh * 4 + ym, 0).start()
            t_copy(k, xh * 4 + ym, 2, d_xh).start()
        else:
            t_copy(k, xh * 4 + ym, 5, d_y[0]).start()

    def t_pass1(k):
        if k in Y_FIRST:
            t_wait(k, 3)
            t_half(k, xh * 4 + yp, 1).start()
            t_copy(k, xh * 4 + yp, 4, d_xh).start()
        else:
            t_wait(k, 4)
            t_copy(k, oh * 4 + yp, 6, d_y[1]).start()

    def t_far(k):
        t_half(k, 0, 0).wait_recv()
        t_half(k, 0, 1).wait_recv()
        t_copy(k, xh * 4 + yo, 7, d_xh).start()

    def t_done(k):
        if k in Y_FIRST:
            t_wait(k, 0, 2, 4, 7)
        else:
            t_wait(k, 3, 2, 5, 6)

    def t_sent(k):
        for i in (0, 1, 2, 3, 4):
            t_copy(k, 0, i, d_xh).wait_send()
        if k in Y_FIRST:
            t_half(k, 0, 0).wait_send()
            t_half(k, 0, 1).wait_send()
            t_copy(k, 0, 7, d_xh).wait_send()
        else:
            t_copy(k, 0, 5, d_xh).wait_send()
            t_copy(k, 0, 6, d_xh).wait_send()

    def w_copy(k, slot, i, dev):
        return rcopy(wg.at[k, c, slot], wg.at[k, c, slot], ws.at[k, i], wr.at[k, i], dev)

    def w_core(k, half):
        return rcopy(wg.at[k, half], wg.at[k, half], ws.at[k, 7], wr.at[k, 7], d_core)

    def w_wait(k, *ids):
        for i in ids:
            w_copy(k, 0, i, d_xl).wait_recv()

    def w_own(k):
        w_copy(k, xl * 4 + z, 0, d_xl).start()
        w_copy(k, xl * 4 + z, 1, d_z[0]).start()
        w_copy(k, xl * 4 + z, 3, d_z[1]).start()

    def w_other(k):
        w_wait(k, 0)
        w_copy(k, ol * 4 + z, 2, d_z[0]).start()
        w_copy(k, ol * 4 + z, 4, d_z[1]).start()

    def w_pass0(k):
        w_wait(k, 1)
        w_copy(k, xl * 4 + zm, 5, d_z[0]).start()

    def w_pass1(k):
        w_wait(k, 4)
        w_copy(k, ol * 4 + zp, 6, d_z[1]).start()

    def w_share(k):
        w_wait(k, 3, 2, 5, 6)
        w_core(k, c).start()

    def w_sent(k):
        for i in range(7):
            w_copy(k, 0, i, d_xl).wait_send()
        w_core(k, c).wait_send()

    def u_core(k):
        return rcopy(tb.at[k, 1 - c], cr.at[k], us.at[k, 0], ur.at[k, 0], d_core)

    def u_far(k, p):
        slot = (ol, xl)[p] * 4 + zo
        return rcopy(tb.at[k, c, slot], zf.at[k, p], us.at[k, 1 + p], ur.at[k, 1 + p], d_z[p])

    def u_near(k, p, a):
        slot = ((ol, xl)[a] * 4) + (zp, zm)[p]
        i = 3 + 2 * p + a
        return rcopy(tb.at[k, c, slot], zn.at[k, p, a], us.at[k, i], ur.at[k, i], d_z[p])

    def u_last(k):
        return rcopy(tb.at[k, c, ol * 4 + z], xlb.at[k], us.at[k, 7], ur.at[k, 7], d_xl)

    def term(k):
        t_done(k)

        def tile(j, carry):
            cols = pl.ds(pl.multiple_of(j * 256, 256), 256)
            left = jnp.concatenate([tg[k, i] for i in range(SEQS)], axis=1)
            out = jnp.dot(left, slope[:, cols], preferred_element_type=F32)
            tb[k, :, :, :, cols] = out.astype(BF).reshape(2, 8, RB, 256)
            return carry

        lax.fori_loop(0, HID // 256, tile, 0)
        u_core(k).start()

    def u_first(k):
        u_core(k).wait_recv()

        def add(i, carry):
            tb[k, c, i] = plus(tb.at[k, c, i], cr.at[k, i]).astype(BF)
            return carry

        lax.fori_loop(0, 8, add, 0)
        u_far(k, 0).start()
        u_far(k, 1).start()
        u_near(k, 0, 1).start()
        u_near(k, 1, 0).start()

    def u_pass(k, p):
        slot = (ol, xl)[p] * 4 + (zp, zm)[p]
        u_far(k, p).wait_recv()
        tb[k, c, slot] = plus(tb.at[k, c, slot], zf.at[k, p]).astype(BF)
        u_near(k, p, p).start()

    def u_cross(k):
        u_near(k, 0, 0).wait_recv()
        u_near(k, 1, 0).wait_recv()
        slot = ol * 4 + z
        tb[k, c, slot] = plus(tb.at[k, c, slot], zn.at[k, 0, 0], zn.at[k, 1, 0]).astype(BF)
        u_last(k).start()

    def u_end(k):
        u_near(k, 0, 1).wait_recv()
        u_near(k, 1, 1).wait_recv()
        u_last(k).wait_recv()
        sum_out[k] = plus(tb.at[k, c, xl * 4 + z], xlb.at[k], zn.at[k, 0, 1], zn.at[k, 1, 1])
        u_core(k).wait_send()
        u_last(k).wait_send()
        for p in range(2):
            u_far(k, p).wait_send()
            u_near(k, p, 0).wait_send()
            u_near(k, p, 1).wait_send()
        w_sent(k)

    def v_far(k, p):
        slot = (oh, xh)[p] * 4 + yo
        return rcopy(ib.at[k, slot], yf.at[k, p], vs.at[k, 1 + p], vr.at[k, 1 + p], d_y[p])

    def v_near(k, p, a):
        slot = (oh, xh)[a] * 4 + (yp, ym)[p]
        i = 3 + 2 * p + a
        return rcopy(ib.at[k, slot], yn.at[k, 2 * p + a], vs.at[k, i], vr.at[k, i], d_y[p])

    def v_last(k):
        return rcopy(ib.at[k, oh * 4 + y], xhb.at[k], vs.at[k, 7], vr.at[k, 7], d_xh)

    def v_four(k):
        return rcopy(ib.at[k, pl.ds(oh * 4, 4)], yn.at[k], vs.at[k, 0], vr.at[k, 0], d_xh)

    def v_half(k, p):
        rows = pl.ds(p * HALF, HALF)
        src = ib.at[k, xh * 4 + yo, rows]
        return rcopy(src, xhb.at[k, rows], vs.at[k, 1 + p], vr.at[k, 1 + p], d_y[p])

    def v_side(k, p, a):
        rows = pl.ds(a * HALF, HALF)
        i = 3 + 2 * p + a
        src = ib.at[k, xh * 4 + (yp, ym)[p], rows]
        return rcopy(src, yf.at[k, p, rows], vs.at[k, i], vr.at[k, i], d_y[p])

    def part(k):
        w_core(k, 1 - c).wait_recv()

        def tile(j, carry):
            rows = pl.ds(pl.multiple_of(j * 256, 256), 256)
            left = wg[k].reshape(CD, HID)
            out = lax.dot_general(
                left, slope[rows, :], (((1,), (1,)), ((), ())), preferred_element_type=F32
            )
            out = (out * D ** (-0.5)).astype(BF)
            ib[k, 2 * j] = out[:, :128]
            ib[k, 2 * j + 1] = out[:, 128:]
            return carry

        lax.fori_loop(0, RT // 256, tile, 0)
        if k in Y_FIRST:
            v_four(k).start()
        else:
            v_far(k, 0).start()
            v_far(k, 1).start()
            v_near(k, 0, 1).start()
            v_near(k, 1, 0).start()

    def v_pass(k, p):
        slot = (oh, xh)[p] * 4 + (yp, ym)[p]
        v_far(k, p).wait_recv()
        ib[k, slot] = plus(ib.at[k, slot], yf.at[k, p]).astype(BF)
        v_near(k, p, p).start()

    def v_first(k):
        v_four(k).wait_recv()

        def add(i, carry):
            ib[k, xh * 4 + i] = plus(ib.at[k, xh * 4 + i], yn.at[k, i]).astype(BF)
            return carry

        lax.fori_loop(0, 4, add, 0)
        v_half(k, 0).start()
        v_half(k, 1).start()
        v_side(k, 0, 1).start()
        v_side(k, 1, 0).start()

    def v_cross(k):
        if k in Y_FIRST:
            for p in range(2):
                rows = pl.ds(p * HALF, HALF)
                slot = xh * 4 + (yp, ym)[p]
                v_half(k, p).wait_recv()
                ib[k, slot, rows] = plus(ib.at[k, slot, rows], xhb.at[k, rows]).astype(BF)
                v_side(k, p, p).start()
        else:
            v_near(k, 0, 0).wait_recv()
            v_near(k, 1, 0).wait_recv()
            slot = oh * 4 + y
            ib[k, slot] = plus(ib.at[k, slot], yn.at[k, 0], yn.at[k, 2]).astype(BF)
            v_last(k).start()

    def v_end(k):
        if k in Y_FIRST:
            for p in range(2):
                v_side(k, p, 0).wait_recv()
                v_side(k, p, 1).wait_recv()
            ig_out[k] = plus(ib.at[k, s], yf.at[k, 0], yf.at[k, 1]).astype(BF)
            v_four(k).wait_send()
            for p in range(2):
                v_half(k, p).wait_send()
                v_side(k, p, 0).wait_send()
                v_side(k, p, 1).wait_send()
        else:
            v_near(k, 0, 1).wait_recv()
            v_near(k, 1, 1).wait_recv()
            v_last(k).wait_recv()
            ig_out[k] = plus(ib.at[k, s], xhb.at[k], yn.at[k, 1], yn.at[k, 3]).astype(BF)
            v_last(k).wait_send()
            for p in range(2):
                v_far(k, p).wait_send()
                v_near(k, p, 0).wait_send()
                v_near(k, p, 1).wait_send()
        t_sent(k)

    def make_slope(i, carry):
        slot = i % 2
        for copy in stage(i, slot):
            copy.wait()
        lin = prev[slot].astype(F32)
        sig = jax.nn.sigmoid(lin)
        rows = pl.ds(pl.multiple_of(i * STAGE, STAGE), STAGE)
        slope[rows, :] = (cotv[slot].astype(F32) * sig * (1.0 + lin * (1.0 - sig))).astype(BF)

        @pl.when(i + 2 < RT // STAGE)
        def _():
            for copy in stage(i + 2, slot):
                copy.start()

        return carry

    work = dict(
        t_cross=t_cross, t_own=t_own, t_other=t_other, t_pass0=t_pass0, t_pass1=t_pass1, t_far=t_far,
        w_own=w_own, w_other=w_other, w_pass0=w_pass0, w_pass1=w_pass1, w_share=w_share,
        term=term, u_first=u_first, u_cross=u_cross, u_end=u_end,
        u_pass0=lambda k: u_pass(k, 0), u_pass1=lambda k: u_pass(k, 1),
        part=part, v_first=v_first, v_cross=v_cross, v_end=v_end,
        v_pass0=lambda k: v_pass(k, 0), v_pass1=lambda k: v_pass(k, 1),
        slope=lambda k: lax.fori_loop(0, RT // STAGE, make_slope, 0),
    )
    for name, k in ORDER:
        work[name](k)


def exchange(tokens, preact, cotangent, master):
    any_spec = pl.BlockSpec(memory_space=pl.ANY)
    vmem = pl.BlockSpec(memory_space=pltpu.VMEM)
    dma = pltpu.SemaphoreType.DMA
    return pl.pallas_call(
        kernel,
        out_shape=(
            jax.ShapeDtypeStruct((CH, RB, HID), F32),
            jax.ShapeDtypeStruct((CH, CD, TOK), BF),
        ),
        in_specs=[any_spec] * 4,
        out_specs=(vmem, vmem),
        scratch_shapes=[
            pltpu.VMEM((CH, SEQS, CD, TOK), BF),
            pltpu.VMEM((CH, 2, 8, RB, HID), BF),
            pltpu.VMEM((RT, HID), BF),
            pltpu.VMEM((CH, 2, 8, RB, HID), BF),
            pltpu.VMEM((CH, 8, RB, HID), BF),
            pltpu.VMEM((CH, 2, RB, HID), BF),
            pltpu.VMEM((CH, 2, 2, RB, HID), BF),
            pltpu.VMEM((CH, RB, HID), BF),
            pltpu.VMEM((CH, SEQS, CD, TOK), BF),
            pltpu.VMEM((CH, 2, CD, TOK), BF),
            pltpu.VMEM((CH, 4, CD, TOK), BF),
            pltpu.VMEM((CH, CD, TOK), BF),
            pltpu.VMEM((TOK, D), BF),
            pltpu.VMEM((CH, RB, HID), F32),
            pltpu.VMEM((2, STAGE, HID), BF),
            pltpu.VMEM((2, STAGE, HID), BF),
            dma((2,)),
            dma((2, 2)),
            *[dma((CH, 8)) for _ in range(8)],
        ],
        compiler_params=pltpu.CompilerParams(
            collective_id=0, has_side_effects=True, vmem_limit_bytes=62 * 2**20
        ),
        cost_estimate=pl.CostEstimate(
            flops=4 * RT * HID * D, bytes_accessed=12 * 2**20, transcendentals=RT * HID
        ),
        name="exchange",
    )(tokens, preact, cotangent, master)


def per_device(tokens, preact, cotangent, master, first_moment, second_moment):
    summed, turned = exchange(tokens, preact, cotangent, master.reshape(CH, RB, HID))
    turned = turned.reshape(CH, 2, 2, 4, RB, TOK)
    input_grad = turned.transpose(5, 2, 3, 1, 0, 4).reshape(TOK, D)
    pseudo = summed.reshape(OWN, HID) * (RT * REGIONS) ** (-0.5)
    new_first = 0.9 * first_moment + 0.1 * pseudo
    new_second = 0.999 * second_moment + 0.001 * pseudo * pseudo
    new_master = master - 0.1 * new_first / (jnp.sqrt(new_second) + 0.001)
    return (new_master, new_first, new_second, input_grad)


def solution(mesh):
    block = P("region", "seq")
    rows = P(("region", "seq"), None)
    return jax.shard_map(
        per_device,
        mesh=mesh,
        in_specs=(rows, block, block, block, block, block),
        out_specs=(block, block, block, rows),
        check_vma=False,
    )
```

time: 148 us -> 123 us (0.83)
  Pallas kernels: 141 us -> 115 us
    pallas_call x1, Pallas kernels: 141 us -> 115 us  [exchange(): pl.pallas_call(kernel, out_shape=(jax.ShapeDtypeStruct((CH, RB, HID), F32...]
where the time goes in v2:
time: 123 us
  Pallas kernels  115 us (93%)
  local copies, waits for them, and re-layouts  4.28 us (3%)
  other arithmetic  2.3 us (2%)
    pallas_call x1, Pallas kernels, exchange(): pl.pallas_call(kernel, out_shape=(jax.ShapeDtypeStruct((CH, RB, HID), F32...  115 us
    unnamed x9, local copies, waits for them, and re-layouts  3.02 us

profile of v2, /device:TPU:0, one launch (start us, length us, event | category | flops | bytes accessed | tf_op | source)
XLA Modules:
  0.0 122.5 jit_solution(1146205606961177398)
XLA Ops:
  0.6 115.3 %exchange.1 = (f32[7,32,1280]{2,1,0:T(8,128)}, bf16[7,512,128]{2,1,0:T(8,128)(2,1)}) custom-call(bf16[128,3584]{1,0:T(8,128)(2,1)} %tok.1, bf16[1024,1280]{1,0:T(8,128)(2,1)} %pre.1, bf16[1024,1280]{1,0:T(8,128)(2,1)} %cot.1, f32[7,32,1280]{2,1,0:T(8,128)} %bitcast.12), custom_call_target="tpu_custom_call" | custom-call | flops 18790481920 | bytes 12582912 | tf_op jit(solution)/shard_map/exchange/pallas_call | solution.py:439
  115.9 1.3 %copy.11 = bf16[7,2,2,4,32,128]{5,4,0,1,3,2:T(8,128)(2,1)S(1)} copy(bf16[7,2,2,4,32,128]{5,4,3,2,1,0:T(8,128)(2,1)} %bitcast.13) | data formatting | bytes 1835008 | tf_op jit(solution)/shard_map/reshape | solution.py:480
  117.2 0.0 copy-start.3
  117.2 1.3 %copy.12 = bf16[128,3584]{1,0:T(8,128)(2,1)} copy(bf16[128,3584]{0,1:T(8,128)(2,1)S(1)} %bitcast.11) | data formatting | bytes 1835008
  118.5 0.0 copy-done.3
  118.5 0.0 copy-start
  118.5 0.0 copy-start.1
  118.5 0.0 copy-start.2
  118.5 0.2 multiply_multiply_fusion
  118.8 1.0 copy-done
  119.8 0.3 copy-done.1
  120.1 0.3 copy-done.2
  120.5 2.0 %divide_subtract_fusion = (f32[224,1280]{1,0:T(8,128)}, f32[224,1280]{1,0:T(8,128)}, f32[224,1280]{1,0:T(8,128)}) fusion(f32[224,1280]{1,0:T(8,128)S(1)} %copy-done, f32[7,32,1280]{2,1,0:T(8,128)S(1)} %get-tuple-element.16, f32[224,1280]{1,0:T(8,128)S(1)} %copy-done.1, f32[7,32,1280]{2,1,0:T(8,128)S(1)} %get-tuple-element.15, f32[224,1280]{1,0:T(8,128)S(1)} %copy-done.2), kind=kLoop, calls=%fused_computation.2 | loop fusion | flops 2293760 | bytes 9175040 | tf_op jit(solution)/shard_map/sub | solution.py:485
Async XLA Ops:
  117.2 1.3 %copy-start.3 = (f32[7,32,1280]{2,1,0:T(8,128)S(1)}, f32[7,32,1280]{2,1,0:T(8,128)}, u32[]{:S(2)}) copy-start(f32[7,32,1280]{2,1,0:T(8,128)} %get-tuple-element.6) | copy-start | bytes 3440644
  118.5 1.3 %copy-start = (f32[224,1280]{1,0:T(8,128)S(1)}, f32[224,1280]{1,0:T(8,128)}, u32[]{:S(2)}) copy-start(f32[224,1280]{1,0:T(8,128)} %param.9) | copy-start | bytes 3440644
  118.5 1.6 %copy-start.1 = (f32[224,1280]{1,0:T(8,128)S(1)}, f32[224,1280]{1,0:T(8,128)}, u32[]{:S(2)}) copy-start(f32[224,1280]{1,0:T(8,128)} %param.10) | copy-start | bytes 3440644
  118.5 1.9 %copy-start.2 = (f32[224,1280]{1,0:T(8,128)S(1)}, f32[224,1280]{1,0:T(8,128)}, u32[]{:S(2)}) copy-start(f32[224,1280]{1,0:T(8,128)} %param.11) | copy-start | bytes 3440644

commit v3 on v2

--- a/solution.py
+++ b/solution.py
@@ -434,16 +434,15 @@
 
 def exchange(tokens, preact, cotangent, master):
     any_spec = pl.BlockSpec(memory_space=pl.ANY)
-    vmem = pl.BlockSpec(memory_space=pltpu.VMEM)
     dma = pltpu.SemaphoreType.DMA
     return pl.pallas_call(
         kernel,
         out_shape=(
-            jax.ShapeDtypeStruct((CH, RB, HID), F32),
-            jax.ShapeDtypeStruct((CH, CD, TOK), BF),
+            pltpu.VMEM((CH, RB, HID), F32),
+            pltpu.VMEM((CH, CD, TOK), BF),
         ),
         in_specs=[any_spec] * 4,
-        out_specs=(vmem, vmem),
+        out_specs=(pl.BlockSpec(memory_space=pltpu.VMEM),) * 2,
         scratch_shapes=[
             pltpu.VMEM((CH, SEQS, CD, TOK), BF),
             pltpu.VMEM((CH, 2, 8, RB, HID), BF),
@@ -466,7 +465,7 @@
             *[dma((CH, 8)) for _ in range(8)],
         ],
         compiler_params=pltpu.CompilerParams(
-            collective_id=0, has_side_effects=True, vmem_limit_bytes=62 * 2**20
+            collective_id=0, has_side_effects=True, vmem_limit_bytes=56 * 2**20
         ),
         cost_estimate=pl.CostEstimate(
             flops=4 * RT * HID * D, bytes_accessed=12 * 2**20, transcendentals=RT * HID
@@ -475,15 +474,71 @@
     )(tokens, preact, cotangent, master)
 
 
+def finish_kernel(
+    summed, turned, mas, first, second, new_mas, new_first, new_second, grad,
+    insv, outv, gradv, in_sem, out_sem, grad_sem,
+):
+    def rows(k):
+        return pl.ds(k * RB, RB)
+
+    def get(k):
+        srcs = (mas.at[rows(k)], first.at[rows(k)], second.at[rows(k)])
+        return [pltpu.make_async_copy(src, insv.at[i, k], in_sem.at[i, k]) for i, src in enumerate(srcs)]
+
+    def put(k):
+        dsts = (new_mas, new_first, new_second)
+        return [
+            pltpu.make_async_copy(outv.at[i, k], dst.at[rows(k)], out_sem.at[i, k]) for i, dst in enumerate(dsts)
+        ]
+
+    put_grad = pltpu.make_async_copy(gradv, grad, grad_sem)
+    for j in range(D // 128):
+        pieces = []
+        for m in range(128 // RB):
+            q, row = place(j * 128 + m * RB)
+            pieces.append(turned[q, row:row + RB, :])
+        gradv[:, j * 128:(j + 1) * 128] = jnp.concatenate(pieces, axis=0).T
+    put_grad.start()
+    for k in range(CH):
+        pseudo = summed[k] * (RT * REGIONS) ** (-0.5)
+        one = 0.9 * first[rows(k), :] + 0.1 * pseudo
+        two = 0.999 * second[rows(k), :] + 0.001 * pseudo * pseudo
+        outv[0, k] = mas[rows(k), :] - 0.1 * one / (jnp.sqrt(two) + 0.001)
+        outv[1, k] = one
+        outv[2, k] = two
+        for copy in put(k):
+            copy.start()
+    put_grad.wait()
+    for k in range(CH):
+        for copy in put(k):
+            copy.wait()
+
+
+def finish(summed, turned, master, first_moment, second_moment):
+    any_spec = pl.BlockSpec(memory_space=pl.ANY)
+    state = jax.ShapeDtypeStruct((OWN, HID), F32)
+    dma = pltpu.SemaphoreType.DMA
+    return pl.pallas_call(
+        finish_kernel,
+        out_shape=(state, state, state, jax.ShapeDtypeStruct((TOK, D), BF)),
+        in_specs=[pl.BlockSpec(memory_space=pltpu.VMEM)] * 5,
+        out_specs=(any_spec,) * 4,
+        scratch_shapes=[
+            pltpu.VMEM((3, CH, RB, HID), F32),
+            pltpu.VMEM((3, CH, RB, HID), F32),
+            pltpu.VMEM((TOK, D), BF),
+            dma((3, CH)),
+            dma((3, CH)),
+            dma,
+        ],
+        compiler_params=pltpu.CompilerParams(vmem_limit_bytes=16 * 2**20),
+        name="finish",
+    )(summed, turned, master, first_moment, second_moment)
+
+
 def per_device(tokens, preact, cotangent, master, first_moment, second_moment):
     summed, turned = exchange(tokens, preact, cotangent, master.reshape(CH, RB, HID))
-    turned = turned.reshape(CH, 2, 2, 4, RB, TOK)
-    input_grad = turned.transpose(5, 2, 3, 1, 0, 4).reshape(TOK, D)
-    pseudo = summed.reshape(OWN, HID) * (RT * REGIONS) ** (-0.5)
-    new_first = 0.9 * first_moment + 0.1 * pseudo
-    new_second = 0.999 * second_moment + 0.001 * pseudo * pseudo
-    new_master = master - 0.1 * new_first / (jnp.sqrt(new_second) + 0.001)
-    return (new_master, new_first, new_second, input_grad)
+    return finish(summed, turned, master, first_moment, second_moment)
 
 
 def solution(mesh):

time: 123 us -> 118 us (0.959)
  local copies, waits for them, and re-layouts: 4.28 us -> 0.01 us
  other arithmetic: 2.3 us -> 0 us
  Pallas kernels: 115 us -> 117 us
    unnamed x9 -> x6, local copies, waits for them, and re-layouts: 3.02 us -> 0.01 us
    sub x1 -> x0, other arithmetic: 2.05 us -> none  [per_device(): new_master = master - 0.1 * new_first / (jnp.sqrt(new_second) + 0.001)]
    pallas_call x1 -> x2, Pallas kernels: 115 us -> 117 us  [the longest x1 114 us: exchange(): pl.pallas_call(kernel, out_shape=(pltpu.VMEM((CH, RB, HID), F32), pltpu.V...]
    reshape x1 -> x0, local copies, waits for them, and re-layouts: 1.26 us -> none  [per_device(): turned = turned.reshape(CH, 2, 2, 4, RB, TOK)]
where the time goes in v3:
time: 118 us; the launch traced here: 117 us
  Pallas kernels  117 us (99%)
    pallas_call x1, Pallas kernels, exchange(): pl.pallas_call(kernel, out_shape=(pltpu.VMEM((CH, RB, HID), F32), pltpu.V...  114 us
    pallas_call x1, Pallas kernels, finish(): pl.pallas_call(finish_kernel, out_shape=(state, state, state, jax.ShapeDt...  2.83 us

profile of v3, /device:TPU:0, one launch (start us, length us, event | category | flops | bytes accessed | tf_op | source)
XLA Modules:
  0.0 117.5 jit_solution(1691073794742836918)
XLA Ops:
  0.6 0.0 copy-start
  0.6 0.0 copy-start.1
  0.7 0.0 copy-start.2
  0.7 114.0 %exchange.1 = (f32[7,32,1280]{2,1,0:T(8,128)S(1)}, bf16[7,512,128]{2,1,0:T(8,128)(2,1)S(1)}) custom-call(bf16[128,3584]{1,0:T(8,128)(2,1)} %tok.1, bf16[1024,1280]{1,0:T(8,128)(2,1)} %pre.1, bf16[1024,1280]{1,0:T(8,128)(2,1)} %cot.1, f32[7,32,1280]{2,1,0:T(8,128)} %bitcast.1), custom_call_target="tpu_custom_call" | custom-call | flops 18790481920 | bytes 12582912 | tf_op jit(solution)/shard_map/exchange/pallas_call | solution.py:438
  114.6 0.0 copy-done
  114.6 0.0 copy-done.1
  114.7 0.0 copy-done.2
  114.7 2.8 %finish.1 = (f32[224,1280]{1,0:T(8,128)}, f32[224,1280]{1,0:T(8,128)}, f32[224,1280]{1,0:T(8,128)}, bf16[128,3584]{1,0:T(8,128)(2,1)}) custom-call(f32[7,32,1280]{2,1,0:T(8,128)S(1)} %get-tuple-element.6.summed, bf16[7,512,128]{2,1,0:T(8,128)(2,1)S(1)} %get-tuple-element.7.turned, f32[224,1280]{1,0:T(8,128)S(1)} %copy-done, f32[224,1280]{1,0:T(8,128)S(1)} %copy-done.1, ...), custom_call_target="tpu_custom_call" | custom-call | tf_op jit(solution)/shard_map/finish/pallas_call | solution.py:521
Async XLA Ops:
  0.6 114.0 %copy-start = (f32[224,1280]{1,0:T(8,128)S(1)}, f32[224,1280]{1,0:T(8,128)}, u32[]{:S(2)}) copy-start(f32[224,1280]{1,0:T(8,128)} %mas.1) | copy-start | bytes 3440644
  0.6 114.0 %copy-start.1 = (f32[224,1280]{1,0:T(8,128)S(1)}, f32[224,1280]{1,0:T(8,128)}, u32[]{:S(2)}) copy-start(f32[224,1280]{1,0:T(8,128)} %first.1) | copy-start | bytes 3440644
  0.7 114.0 %copy-start.2 = (f32[224,1280]{1,0:T(8,128)S(1)}, f32[224,1280]{1,0:T(8,128)}, u32[]{:S(2)}) copy-start(f32[224,1280]{1,0:T(8,128)} %second.1) | copy-start | bytes 3440644

commit v4 on v3

v4 whole, which is shorter than its diff:
```python
import jax
import jax.numpy as jnp
from jax import lax
from jax.experimental import pallas as pl
from jax.experimental.pallas import tpu as pltpu
from jax.sharding import PartitionSpec as P

MESH = pl.DeviceIdType.MESH
BF = jnp.bfloat16
F32 = jnp.float32

D = 3584
REGIONS = 16
SEQS = 8
OWN = D // REGIONS
CH = 7
RB = OWN // CH
CD = D // CH
HALF = CD // 2
TOK = 128
HID = 1280
RT = TOK * SEQS
STAGE = 128
ST = RT // STAGE
HT = RT // 2
X_FIRST = (3, 5)
Z_FIRST = tuple(k for k in range(CH) if k not in X_FIRST)

(
    T_OWN, T_PASS0, T_PASS1, T_SHARE, W_OWN, W_OTHER, W_PASS0, W_PASS1, W_SHARE,
    SLOPE0, SLOPE1, S_CROSS, S_PASS, TERM0, TERM1, U_PASS0, U_PASS1, U_TURN,
    U_XPASS0, U_XPASS1, U_END, PART, V_PASS0, V_PASS1, V_CROSS, V_END,
) = range(26)
ORDER = (
    (W_OWN, 3), (T_OWN, 0), (T_OWN, 1), (W_OWN, 6), (SLOPE0, 0), (T_OWN, 3), (W_OWN, 0), (W_OWN, 4),
    (W_OTHER, 3), (W_OTHER, 6), (T_OWN, 4), (W_OWN, 2), (W_PASS0, 3), (S_CROSS, 0), (W_PASS0, 6),
    (T_OWN, 5), (W_OWN, 1), (S_CROSS, 3), (T_PASS0, 1), (SLOPE1, 0), (T_PASS1, 4), (S_CROSS, 2),
    (W_PASS1, 6), (T_OWN, 2), (W_PASS0, 4), (S_CROSS, 1), (W_OTHER, 4), (T_PASS0, 0), (T_PASS1, 3),
    (W_PASS0, 0), (T_PASS1, 0), (W_OTHER, 0), (T_PASS1, 1), (W_SHARE, 6), (W_PASS1, 4), (T_PASS1, 2),
    (T_PASS0, 4), (W_PASS0, 1), (W_PASS1, 0), (T_PASS0, 5), (W_OTHER, 1), (W_SHARE, 4), (T_PASS0, 2),
    (T_PASS1, 5), (W_OWN, 5), (T_PASS0, 3), (T_SHARE, 4), (PART, 6), (W_PASS1, 3), (T_SHARE, 2),
    (T_SHARE, 5), (W_OTHER, 2), (T_SHARE, 0), (T_SHARE, 1), (TERM0, 4), (PART, 4), (TERM0, 2), (T_SHARE, 3),
    (W_SHARE, 3), (TERM0, 5), (TERM0, 1), (V_PASS0, 6), (V_PASS1, 4), (W_PASS0, 5), (W_SHARE, 0),
    (W_PASS0, 2), (V_PASS0, 4), (T_OWN, 6), (TERM0, 0), (S_PASS, 0), (V_PASS1, 6), (V_CROSS, 6),
    (U_PASS1, 4), (W_PASS1, 2), (PART, 0), (V_CROSS, 4), (W_OTHER, 5), (T_PASS1, 6), (TERM1, 5), (TERM1, 4),
    (PART, 3), (TERM1, 2), (W_SHARE, 2), (U_XPASS0, 5), (W_PASS1, 5), (U_XPASS1, 5), (TERM0, 3),
    (V_PASS0, 0), (W_PASS1, 1), (U_PASS1, 1), (U_PASS0, 4), (TERM1, 3), (V_PASS0, 3), (V_PASS1, 3),
    (U_PASS0, 2), (PART, 2), (TERM1, 1), (W_SHARE, 5), (V_CROSS, 0), (TERM1, 0), (U_PASS1, 2), (T_PASS0, 6),
    (V_PASS1, 0), (U_TURN, 4), (PART, 5), (V_PASS1, 2), (U_PASS0, 1), (W_SHARE, 1), (V_CROSS, 3),
    (U_XPASS1, 4), (U_PASS1, 0), (T_SHARE, 6), (U_XPASS1, 3), (U_PASS0, 0), (U_XPASS0, 3), (U_XPASS0, 4),
    (V_PASS0, 5), (V_PASS0, 2), (TERM0, 6), (U_TURN, 1), (TERM1, 6), (U_TURN, 0), (U_TURN, 2), (V_CROSS, 5),
    (PART, 1), (U_PASS1, 6), (V_CROSS, 2), (U_PASS0, 6), (U_XPASS1, 2), (U_XPASS1, 1), (V_PASS1, 5),
    (U_XPASS1, 0), (U_TURN, 3), (U_TURN, 5), (U_XPASS0, 2), (U_XPASS0, 0), (V_PASS0, 1), (U_XPASS0, 1),
    (U_PASS1, 3), (U_TURN, 6), (V_PASS1, 1), (V_END, 3), (V_END, 2), (V_CROSS, 1), (U_END, 4), (U_PASS0, 5),
    (V_END, 0), (V_END, 4), (U_PASS0, 3), (U_XPASS0, 6), (U_PASS1, 5), (U_END, 2), (U_XPASS1, 6),
    (U_END, 0), (V_END, 6), (V_END, 5), (U_END, 5), (U_END, 3), (U_END, 1), (V_END, 1), (U_END, 6),
)

FIRST0 = next(k for name, k in ORDER if name == TERM0)
FIRST1 = next(k for name, k in ORDER if name == TERM1)


def place(d0):
    owner, rest = divmod(d0, OWN)
    k, i = divmod(rest, RB)
    xl, z, c = owner // 8, owner // 2 % 4, owner % 2
    return k, ((c * 4 + z) * 2 + xl) * RB + i


def rcopy(src, dst, send, recv, dev):
    return pltpu.make_async_remote_copy(
        src_ref=src, dst_ref=dst, send_sem=send, recv_sem=recv, device_id=dev, device_id_type=MESH
    )


def plus(*refs):
    total = refs[0][...].astype(F32)
    for ref in refs[1:]:
        total = total + ref[...].astype(F32)
    return total


def kernel(
    tok, pre, cot, mas, sum_out, ig_out,
    tg, tc, wg, slope, sx, tb, zf, zn, xf, xs, xf4, xs4, zf1, zs1, ib, yf, yn, xhb, tokv, masv, prev, cotv,
    in_sem, st_sem, ts, tr, ws, wr, us, ur, vs, vr, ss, sr,
):
    r = lax.axis_index("region")
    s = lax.axis_index("seq")
    xl, z, c = r // 8, (r // 2) % 4, r % 2
    xh, y = s // 4, s % 4
    ol, oh = 1 - xl, 1 - xh
    zp, zm, zo = (z + 1) % 4, (z + 3) % 4, (z + 2) % 4
    yp, ym, yo = (y + 1) % 4, (y + 3) % 4, (y + 2) % 4

    def device(a, b, d, e, f):
        return (a * 8 + b * 2 + d, e * 4 + f)

    d_core = device(xl, z, 1 - c, xh, y)
    d_x = (device(ol, z, c, xh, y), device(ol, z, c, oh, y))
    d_xh = device(xl, z, c, oh, y)
    d_z = (device(xl, zp, c, xh, y), device(xl, zm, c, xh, y))
    d_y = (device(xl, z, c, xh, yp), device(xl, z, c, xh, ym))

    get_tok = pltpu.make_async_copy(tok, tokv, in_sem.at[0])
    get_mas = pltpu.make_async_copy(mas, masv, in_sem.at[1])
    get_tok.start()
    get_mas.start()

    def stage(i, slot):
        half = oh + (i // 4) * (xh - oh)
        rows = pl.ds(pl.multiple_of((half * 4 + i % 4) * STAGE, STAGE), STAGE)
        return rows, (
            pltpu.make_async_copy(pre.at[rows], prev.at[slot], st_sem.at[0, slot]),
            pltpu.make_async_copy(cot.at[rows], cotv.at[slot], st_sem.at[1, slot]),
        )

    for i in range(2):
        for copy in stage(i, i)[1]:
            copy.start()

    barrier = pltpu.get_barrier_semaphore()
    for dev in (d_core, *d_x, d_xh, *d_z, *d_y):
        pl.semaphore_signal(barrier, inc=1, device_id=dev, device_id_type=MESH)

    get_tok.wait()
    for j in range(D // 128):
        turned = tokv[:, j * 128:(j + 1) * 128].T
        for m in range(128 // RB):
            k, row = place(j * 128 + m * RB)
            half, row = divmod(row, HALF)
            tg[k, y, half, row:row + RB, :] = turned[m * RB:(m + 1) * RB, :]
    pl.semaphore_wait(barrier, 8)

    def t_copy(k, slot, i):
        return rcopy(tg.at[k, slot], tg.at[k, slot], ts.at[k, i], tr.at[k, i], d_y[i])

    def t_half(k, slot, p):
        return rcopy(tg.at[k, slot, p], tg.at[k, slot, p], ts.at[k, 2 + p], tr.at[k, 2 + p], d_y[p])

    def t_core(k):
        return rcopy(tg.at[k, :, 1 - c], tc.at[k], ts.at[k, 4], tr.at[k, 4], d_core)

    def t_own(k):
        t_copy(k, y, 0).start()
        t_copy(k, y, 1).start()

    def t_pass(k, p):
        t_copy(k, y, p).wait_recv()
        t_half(k, (ym, yp)[p], p).start()

    def t_share(k):
        t_half(k, yo, 0).wait_recv()
        t_half(k, yo, 1).wait_recv()
        t_core(k).start()

    def t_sent(k):
        for p in range(2):
            t_copy(k, y, p).wait_send()
            t_half(k, y, p).wait_send()
        t_core(k).wait_send()

    def w_copy(k, slot, i, dev):
        return rcopy(wg.at[k, c, slot], wg.at[k, c, slot], ws.at[k, i], wr.at[k, i], dev)

    def w_core(k, half):
        return rcopy(wg.at[k, half], wg.at[k, half], ws.at[k, 7], wr.at[k, 7], d_core)

    def w_wait(k, *ids):
        for i in ids:
            w_copy(k, 0, i, d_x[0]).wait_recv()

    def w_own(k):
        wg[k, c, z * 2 + xl] = masv[k].astype(BF)
        w_copy(k, z * 2 + xl, 0, d_x[0]).start()
        w_copy(k, z * 2 + xl, 1, d_z[0]).start()
        w_copy(k, z * 2 + xl, 3, d_z[1]).start()

    def w_other(k):
        w_wait(k, 0)
        w_copy(k, z * 2 + ol, 2, d_z[0]).start()
        w_copy(k, z * 2 + ol, 4, d_z[1]).start()

    def w_pass0(k):
        w_wait(k, 1)
        w_copy(k, zm * 2 + xl, 5, d_z[0]).start()

    def w_pass1(k):
        w_wait(k, 4)
        w_copy(k, zp * 2 + ol, 6, d_z[1]).start()

    def w_share(k):
        w_wait(k, 3, 2, 5, 6)
        w_core(k, c).start()

    def w_sent(k):
        for i in range(7):
            w_copy(k, 0, i, d_x[0]).wait_send()
        w_core(k, c).wait_send()

    def make_slope(i, carry):
        slot = i % 2
        rows, copies = stage(i, slot)
        for copy in copies:
            copy.wait()
        lin = prev[slot].astype(F32)
        sig = jax.nn.sigmoid(lin)
        slope[rows, :] = (cotv[slot].astype(F32) * sig * (1.0 + lin * (1.0 - sig))).astype(BF)

        @pl.when(i + 2 < ST)
        def _():
            for copy in stage(i + 2, slot)[1]:
                copy.start()

        return carry

    def own_rows():
        return pl.ds(pl.multiple_of(xh * HT, HT), HT)

    def s_copy(i):
        rows = pl.ds(pl.multiple_of((oh * 4 + i) * STAGE, STAGE), STAGE)
        return rcopy(slope.at[rows], sx.at[0, pl.ds(i * STAGE, STAGE)], ss.at[i], sr.at[i], d_xh)

    def s_core(i):
        src = (slope.at[own_rows()], sx.at[0])[i]
        return rcopy(src, sx.at[1 + i], ss.at[4 + i], sr.at[4 + i], d_core)

    def slope0(k):
        lax.fori_loop(0, ST // 2, make_slope, 0)

    def slope1(k):
        lax.fori_loop(ST // 2, ST, make_slope, 0)
        s_core(0).start()

    def s_cross(i):
        s_copy(i).start()

    def s_pass(k):
        for i in range(4):
            s_copy(i).wait_recv()
        s_core(1).start()

    def s_sent():
        for i in range(4):
            s_copy(i).wait_send()
        s_core(0).wait_send()
        s_core(1).wait_send()

    def u_copy(k, i, src, dst, dev):
        return rcopy(src, dst, us.at[k, i], ur.at[k, i], dev)

    def half_rows(a):
        return pl.ds(a * (RB // 2), RB // 2)

    def u_far(k, p):
        if k in X_FIRST:
            n = X_FIRST.index(k)
            src, dst = tb.at[k, zo, 0, xl, half_rows(p)], zf1.at[n, half_rows(p)]
        else:
            n = Z_FIRST.index(k)
            src, dst = tb.at[k, zo, 1 - p], zf.at[n, p]
        return u_copy(k, p, src, dst, d_z[p])

    def u_near(k, p, a):
        slot = (zp, zm)[p]
        if k in X_FIRST:
            n = X_FIRST.index(k)
            src, dst = tb.at[k, slot, 0, xl, half_rows(a)], zs1.at[n, p, half_rows(a)]
        else:
            n = Z_FIRST.index(k)
            src, dst = tb.at[k, slot, a], zn.at[n, p, a]
        return u_copy(k, 2 + 2 * p + a, src, dst, d_z[p])

    def u_xfar(k, p):
        if k in X_FIRST:
            n = X_FIRST.index(k)
            src, dst = tb.at[k, :, 1, xl, half_rows(p)], xf4.at[n, :, half_rows(p)]
        else:
            n = Z_FIRST.index(k)
            src, dst = tb.at[k, z, 1, xl, half_rows(p)], xf.at[n, half_rows(p)]
        return u_copy(k, 6 + p, src, dst, d_x[p])

    def u_xnear(k, p, a):
        if k in X_FIRST:
            n = X_FIRST.index(k)
            src, dst = tb.at[k, :, p, ol, half_rows(a)], xs4.at[n, p, :, half_rows(a)]
        else:
            n = Z_FIRST.index(k)
            src, dst = tb.at[k, z, p, ol, half_rows(a)], xs.at[n, p, half_rows(a)]
        return u_copy(k, 8 + 2 * p + a, src, dst, d_x[p])

    def term(k, h):
        if h == 0:
            t_core(k).wait_recv()
            if k == FIRST0:
                s_core(0).wait_recv()
        elif k == FIRST1:
            s_core(1).wait_recv()

        def tile(j, carry):
            cols = pl.ds(pl.multiple_of(j * 256, 256), 256)
            mine = jnp.concatenate([tg[k, i, c] for i in range(4)], axis=1)
            theirs = jnp.concatenate([tc[k, i] for i in range(4)], axis=1)
            own = slope[own_rows(), cols] if h == 0 else sx[0, :, cols]
            out = jnp.dot(mine, own, preferred_element_type=F32)
            out = out + jnp.dot(theirs, sx[1 + h, :, cols], preferred_element_type=F32)
            tb[k, :, h, :, :, cols] = out.astype(BF).reshape(4, 2, RB, 256)
            return carry

        lax.fori_loop(0, HID // 256, tile, 0)
        if k in Z_FIRST:
            u_far(k, 1 - h).start()
            u_near(k, h, h).start()
        elif h == 1:
            u_xsend(k)

    def u_xsend(k):
        u_xfar(k, 0).start()
        u_xfar(k, 1).start()
        u_xnear(k, 0, 0).start()
        u_xnear(k, 1, 1).start()

    def u_pass(k, p):
        u_far(k, p).wait_recv()
        slot = (zp, zm)[p]
        if k in X_FIRST:
            n = X_FIRST.index(k)
            rows = half_rows(p)
            tb[k, slot, 0, xl, rows] = plus(tb.at[k, slot, 0, xl, rows], zf1.at[n, rows]).astype(BF)
            u_near(k, p, p).start()
        else:
            n = Z_FIRST.index(k)
            tb[k, slot, 1 - p] = plus(tb.at[k, slot, 1 - p], zf.at[n, p]).astype(BF)
            u_near(k, p, 1 - p).start()

    def u_turn(k):
        if k in X_FIRST:
            n = X_FIRST.index(k)
            for p in range(2):
                for a in range(2):
                    u_xnear(k, p, a).wait_recv()
            for i in range(4):
                tb[k, i, 0, xl] = plus(tb.at[k, i, 0, xl], xs4.at[n, 0, i], xs4.at[n, 1, i]).astype(BF)
            u_far(k, 0).start()
            u_far(k, 1).start()
            u_near(k, 0, 1).start()
            u_near(k, 1, 0).start()
        else:
            n = Z_FIRST.index(k)
            for p in range(2):
                for a in range(2):
                    u_near(k, p, a).wait_recv()
            for h, a in ((1, xl), (0, ol), (1, ol)):
                tb[k, z, h, a] = plus(tb.at[k, z, h, a], zn.at[n, 0, h, a], zn.at[n, 1, h, a]).astype(BF)
            u_xsend(k)

    def u_xpass(k, p):
        u_xfar(k, p).wait_recv()
        rows = half_rows(p)
        if k in X_FIRST:
            n = X_FIRST.index(k)
            for i in range(4):
                to = tb.at[k, i, 1 - p, ol, rows]
                to[...] = plus(to, xf4.at[n, i, rows]).astype(BF)
        else:
            n = Z_FIRST.index(k)
            to = tb.at[k, z, 1 - p, ol, rows]
            to[...] = plus(to, xf.at[n, rows]).astype(BF)
        u_xnear(k, 1 - p, p).start()

    def u_end(k):
        if k in X_FIRST:
            n = X_FIRST.index(k)
            for p in range(2):
                for a in range(2):
                    u_near(k, p, a).wait_recv()
            sum_out[k] = plus(tb.at[k, z, 0, xl], zs1.at[n, 0], zs1.at[n, 1])
        else:
            n = Z_FIRST.index(k)
            for p in range(2):
                for a in range(2):
                    u_xnear(k, p, a).wait_recv()
            sum_out[k] = plus(
                tb.at[k, z, 0, xl], zn.at[n, 0, 0, xl], zn.at[n, 1, 0, xl], xs.at[n, 0], xs.at[n, 1]
            )
        for p in range(2):
            u_far(k, p).wait_send()
            u_xfar(k, p).wait_send()
            for a in range(2):
                u_near(k, p, a).wait_send()
                u_xnear(k, p, a).wait_send()
        t_sent(k)

    def v_far(k, p):
        slot = (oh, xh)[p] * 4 + yo
        return rcopy(ib.at[k, slot], yf.at[k, p], vs.at[k, 1 + p], vr.at[k, 1 + p], d_y[p])

    def v_near(k, p, a):
        slot = (oh, xh)[a] * 4 + (yp, ym)[p]
        i = 3 + 2 * p + a
        return rcopy(ib.at[k, slot], yn.at[k, 2 * p + a], vs.at[k, i], vr.at[k, i], d_y[p])

    def v_last(k):
        return rcopy(ib.at[k, oh * 4 + y], xhb.at[k], vs.at[k, 7], vr.at[k, 7], d_xh)

    def part(k):
        w_core(k, 1 - c).wait_recv()

        def tile(j, carry):
            rows = pl.ds(pl.multiple_of(j * 256, 256), 256)
            left = wg[k].reshape(CD, HID)
            out = lax.dot_general(
                left, slope[rows, :], (((1,), (1,)), ((), ())), preferred_element_type=F32
            )
            out = (out * D ** (-0.5)).astype(BF)
            ib[k, 2 * j] = out[:, :128]
            ib[k, 2 * j + 1] = out[:, 128:]
            return carry

        lax.fori_loop(0, RT // 256, tile, 0)
        v_far(k, 0).start()
        v_far(k, 1).start()
        v_near(k, 0, 1).start()
        v_near(k, 1, 0).start()

    def v_pass(k, p):
        slot = (oh, xh)[p] * 4 + (yp, ym)[p]
        v_far(k, p).wait_recv()
        ib[k, slot] = plus(ib.at[k, slot], yf.at[k, p]).astype(BF)
        v_near(k, p, p).start()

    def v_cross(k):
        v_near(k, 0, 0).wait_recv()
        v_near(k, 1, 0).wait_recv()
        slot = oh * 4 + y
        ib[k, slot] = plus(ib.at[k, slot], yn.at[k, 0], yn.at[k, 2]).astype(BF)
        v_last(k).start()

    def v_end(k):
        v_near(k, 0, 1).wait_recv()
        v_near(k, 1, 1).wait_recv()
        v_last(k).wait_recv()
        ig_out[k] = plus(ib.at[k, s], xhb.at[k], yn.at[k, 1], yn.at[k, 3]).astype(BF)
        v_last(k).wait_send()
        for p in range(2):
            v_far(k, p).wait_send()
            v_near(k, p, 0).wait_send()
            v_near(k, p, 1).wait_send()
        w_sent(k)

    def both(work):
        return lambda k: work(k, 0), lambda k: work(k, 1)

    t_pass0, t_pass1 = both(t_pass)
    u_pass0, u_pass1 = both(u_pass)
    u_xpass0, u_xpass1 = both(u_xpass)
    v_pass0, v_pass1 = both(v_pass)
    term0, term1 = both(term)
    work = {
        T_OWN: t_own, T_PASS0: t_pass0, T_PASS1: t_pass1, T_SHARE: t_share,
        W_OWN: w_own, W_OTHER: w_other, W_PASS0: w_pass0, W_PASS1: w_pass1,
        W_SHARE: w_share, SLOPE0: slope0, SLOPE1: slope1, S_CROSS: s_cross,
        S_PASS: s_pass, TERM0: term0, TERM1: term1, U_PASS0: u_pass0,
        U_PASS1: u_pass1, U_TURN: u_turn, U_XPASS0: u_xpass0, U_XPASS1: u_xpass1,
        U_END: u_end, PART: part, V_PASS0: v_pass0, V_PASS1: v_pass1,
        V_CROSS: v_cross, V_END: v_end,
    }
    waited = False
    for name, k in ORDER:
        if name == W_OWN and not waited:
            get_mas.wait()
            waited = True
        work[name](k)
    s_sent()


def exchange(tokens, preact, cotangent, master):
    any_spec = pl.BlockSpec(memory_space=pl.ANY)
    dma = pltpu.SemaphoreType.DMA
    return pl.pallas_call(
        kernel,
        out_shape=(
            pltpu.VMEM((CH, RB, HID), F32),
            pltpu.VMEM((CH, CD, TOK), BF),
        ),
        in_specs=[any_spec] * 4,
        out_specs=(pl.BlockSpec(memory_space=pltpu.VMEM),) * 2,
        scratch_shapes=[
            pltpu.VMEM((CH, 4, 2, HALF, TOK), BF),
            pltpu.VMEM((CH, 4, HALF, TOK), BF),
            pltpu.VMEM((CH, 2, 8, RB, HID), BF),
            pltpu.VMEM((RT, HID), BF),
            pltpu.VMEM((3, HT, HID), BF),
            pltpu.VMEM((CH, 4, 2, 2, RB, HID), BF),
            pltpu.VMEM((len(Z_FIRST), 2, 2, RB, HID), BF),
            pltpu.VMEM((len(Z_FIRST), 2, 2, 2, RB, HID), BF),
            pltpu.VMEM((len(Z_FIRST), RB, HID), BF),
            pltpu.VMEM((len(Z_FIRST), 2, RB, HID), BF),
            pltpu.VMEM((len(X_FIRST), 4, RB, HID), BF),
            pltpu.VMEM((len(X_FIRST), 2, 4, RB, HID), BF),
            pltpu.VMEM((len(X_FIRST), RB, HID), BF),
            pltpu.VMEM((len(X_FIRST), 2, RB, HID), BF),
            pltpu.VMEM((CH, SEQS, CD, TOK), BF),
            pltpu.VMEM((CH, 2, CD, TOK), BF),
            pltpu.VMEM((CH, 4, CD, TOK), BF),
            pltpu.VMEM((CH, CD, TOK), BF),
            pltpu.VMEM((TOK, D), BF),
            pltpu.VMEM((CH, RB, HID), F32),
            pltpu.VMEM((2, STAGE, HID), BF),
            pltpu.VMEM((2, STAGE, HID), BF),
            dma((2,)),
            dma((2, 2)),
            dma((CH, 5)),
            dma((CH, 5)),
            dma((CH, 8)),
            dma((CH, 8)),
            dma((CH, 12)),
            dma((CH, 12)),
            dma((CH, 8)),
            dma((CH, 8)),
            dma((6,)),
            dma((6,)),
        ],
        compiler_params=pltpu.CompilerParams(
            collective_id=0, has_side_effects=True, vmem_limit_bytes=56 * 2**20
        ),
        cost_estimate=pl.CostEstimate(
            flops=4 * RT * HID * D, bytes_accessed=12 * 2**20, transcendentals=RT * HID
        ),
        name="exchange",
    )(tokens, preact, cotangent, master)


def finish_kernel(
    summed, turned, mas, first, second, new_mas, new_first, new_second, grad,
    insv, outv, gradv, in_sem, out_sem, grad_sem,
):
    def rows(k):
        return pl.ds(k * RB, RB)

    def get(k):
        srcs = (mas.at[rows(k)], first.at[rows(k)], second.at[rows(k)])
        return [pltpu.make_async_copy(src, insv.at[i, k], in_sem.at[i, k]) for i, src in enumerate(srcs)]

    def put(k):
        dsts = (new_mas, new_first, new_second)
        return [
            pltpu.make_async_copy(outv.at[i, k], dst.at[rows(k)], out_sem.at[i, k]) for i, dst in enumerate(dsts)
        ]

    put_grad = pltpu.make_async_copy(gradv, grad, grad_sem)
    for j in range(D // 128):
        pieces = []
        for m in range(128 // RB):
            q, row = place(j * 128 + m * RB)
            pieces.append(turned[q, row:row + RB, :])
        gradv[:, j * 128:(j + 1) * 128] = jnp.concatenate(pieces, axis=0).T
    put_grad.start()
    for k in range(CH):
        pseudo = summed[k] * (RT * REGIONS) ** (-0.5)
        one = 0.9 * first[rows(k), :] + 0.1 * pseudo
        two = 0.999 * second[rows(k), :] + 0.001 * pseudo * pseudo
        outv[0, k] = mas[rows(k), :] - 0.1 * one / (jnp.sqrt(two) + 0.001)
        outv[1, k] = one
        outv[2, k] = two
        for copy in put(k):
            copy.start()
    put_grad.wait()
    for k in range(CH):
        for copy in put(k):
            copy.wait()


def finish(summed, turned, master, first_moment, second_moment):
    any_spec = pl.BlockSpec(memory_space=pl.ANY)
    state = jax.ShapeDtypeStruct((OWN, HID), F32)
    dma = pltpu.SemaphoreType.DMA
    return pl.pallas_call(
        finish_kernel,
        out_shape=(state, state, state, jax.ShapeDtypeStruct((TOK, D), BF)),
        in_specs=[pl.BlockSpec(memory_space=pltpu.VMEM)] * 5,
        out_specs=(any_spec,) * 4,
        scratch_shapes=[
            pltpu.VMEM((3, CH, RB, HID), F32),
            pltpu.VMEM((3, CH, RB, HID), F32),
            pltpu.VMEM((TOK, D), BF),
            dma((3, CH)),
            dma((3, CH)),
            dma,
        ],
        compiler_params=pltpu.CompilerParams(vmem_limit_bytes=16 * 2**20),
        name="finish",
    )(summed, turned, master, first_moment, second_moment)


def per_device(tokens, preact, cotangent, master, first_moment, second_moment):
    summed, turned = exchange(tokens, preact, cotangent, master.reshape(CH, RB, HID))
    return finish(summed, turned, master, first_moment, second_moment)


def solution(mesh):
    block = P("region", "seq")
    rows = P(("region", "seq"), None)
    return jax.shard_map(
        per_device,
        mesh=mesh,
        in_specs=(rows, block, block, block, block, block),
        out_specs=(block, block, block, rows),
        check_vma=False,
    )
```

time: 118 us -> 116 us (0.983)
  Pallas kernels: 117 us -> 115 us
    pallas_call x1, Pallas kernels: 114 us -> 112 us  [exchange(): pl.pallas_call(kernel, out_shape=(pltpu.VMEM((CH, RB, HID), F32), pltpu.V...]
where the time goes in v4:
time: 116 us
  Pallas kernels  115 us (99%)
    pallas_call x1, Pallas kernels, exchange(): pl.pallas_call(kernel, out_shape=(pltpu.VMEM((CH, RB, HID), F32), pltpu.V...  112 us
    pallas_call x1, Pallas kernels, finish(): pl.pallas_call(finish_kernel, out_shape=(state, state, state, jax.ShapeDt...  2.83 us

profile of v4, /device:TPU:0, one launch (start us, length us, event | category | flops | bytes accessed | tf_op | source)
XLA Modules:
  0.0 116.1 jit_solution(2265791635983069212)
XLA Ops:
  0.6 0.0 copy-start
  0.6 0.0 copy-start.1
  0.7 0.0 copy-start.2
  0.7 112.4 %exchange.1 = (f32[7,32,1280]{2,1,0:T(8,128)S(1)}, bf16[7,512,128]{2,1,0:T(8,128)(2,1)S(1)}) custom-call(bf16[128,3584]{1,0:T(8,128)(2,1)} %tok.1, bf16[1024,1280]{1,0:T(8,128)(2,1)} %pre.1, bf16[1024,1280]{1,0:T(8,128)(2,1)} %cot.1, f32[7,32,1280]{2,1,0:T(8,128)} %bitcast.1), custom_call_target="tpu_custom_call" | custom-call | flops 18790481920 | bytes 12582912 | tf_op jit(solution)/shard_map/exchange/pallas_call | solution.py:480
  113.1 0.0 copy-done
  113.1 0.0 copy-done.1
  113.1 0.0 copy-done.2
  113.1 2.8 %finish.1 = (f32[224,1280]{1,0:T(8,128)}, f32[224,1280]{1,0:T(8,128)}, f32[224,1280]{1,0:T(8,128)}, bf16[128,3584]{1,0:T(8,128)(2,1)}) custom-call(f32[7,32,1280]{2,1,0:T(8,128)S(1)} %get-tuple-element.6.summed, bf16[7,512,128]{2,1,0:T(8,128)(2,1)S(1)} %get-tuple-element.7.turned, f32[224,1280]{1,0:T(8,128)S(1)} %copy-done, f32[224,1280]{1,0:T(8,128)S(1)} %copy-done.1, ...), custom_call_target="tpu_custom_call" | custom-call | tf_op jit(solution)/shard_map/finish/pallas_call | solution.py:578
Async XLA Ops:
  0.6 112.5 %copy-start = (f32[224,1280]{1,0:T(8,128)S(1)}, f32[224,1280]{1,0:T(8,128)}, u32[]{:S(2)}) copy-start(f32[224,1280]{1,0:T(8,128)} %mas.1) | copy-start | bytes 3440644
  0.6 112.5 %copy-start.1 = (f32[224,1280]{1,0:T(8,128)S(1)}, f32[224,1280]{1,0:T(8,128)}, u32[]{:S(2)}) copy-start(f32[224,1280]{1,0:T(8,128)} %first.1) | copy-start | bytes 3440644
  0.7 112.5 %copy-start.2 = (f32[224,1280]{1,0:T(8,128)S(1)}, f32[224,1280]{1,0:T(8,128)}, u32[]{:S(2)}) copy-start(f32[224,1280]{1,0:T(8,128)} %second.1) | copy-start | bytes 3440644

commit v5 on v4

--- a/solution.py
+++ b/solution.py
@@ -23,7 +23,7 @@
 STAGE = 128
 ST = RT // STAGE
 HT = RT // 2
-X_FIRST = (3, 5)
+X_FIRST = (0, 2)
 Z_FIRST = tuple(k for k in range(CH) if k not in X_FIRST)
 
 (
@@ -32,28 +32,29 @@
     U_XPASS0, U_XPASS1, U_END, PART, V_PASS0, V_PASS1, V_CROSS, V_END,
 ) = range(26)
 ORDER = (
-    (W_OWN, 3), (T_OWN, 0), (T_OWN, 1), (W_OWN, 6), (SLOPE0, 0), (T_OWN, 3), (W_OWN, 0), (W_OWN, 4),
-    (W_OTHER, 3), (W_OTHER, 6), (T_OWN, 4), (W_OWN, 2), (W_PASS0, 3), (S_CROSS, 0), (W_PASS0, 6),
-    (T_OWN, 5), (W_OWN, 1), (S_CROSS, 3), (T_PASS0, 1), (SLOPE1, 0), (T_PASS1, 4), (S_CROSS, 2),
-    (W_PASS1, 6), (T_OWN, 2), (W_PASS0, 4), (S_CROSS, 1), (W_OTHER, 4), (T_PASS0, 0), (T_PASS1, 3),
-    (W_PASS0, 0), (T_PASS1, 0), (W_OTHER, 0), (T_PASS1, 1), (W_SHARE, 6), (W_PASS1, 4), (T_PASS1, 2),
-    (T_PASS0, 4), (W_PASS0, 1), (W_PASS1, 0), (T_PASS0, 5), (W_OTHER, 1), (W_SHARE, 4), (T_PASS0, 2),
-    (T_PASS1, 5), (W_OWN, 5), (T_PASS0, 3), (T_SHARE, 4), (PART, 6), (W_PASS1, 3), (T_SHARE, 2),
-    (T_SHARE, 5), (W_OTHER, 2), (T_SHARE, 0), (T_SHARE, 1), (TERM0, 4), (PART, 4), (TERM0, 2), (T_SHARE, 3),
-    (W_SHARE, 3), (TERM0, 5), (TERM0, 1), (V_PASS0, 6), (V_PASS1, 4), (W_PASS0, 5), (W_SHARE, 0),
-    (W_PASS0, 2), (V_PASS0, 4), (T_OWN, 6), (TERM0, 0), (S_PASS, 0), (V_PASS1, 6), (V_CROSS, 6),
-    (U_PASS1, 4), (W_PASS1, 2), (PART, 0), (V_CROSS, 4), (W_OTHER, 5), (T_PASS1, 6), (TERM1, 5), (TERM1, 4),
-    (PART, 3), (TERM1, 2), (W_SHARE, 2), (U_XPASS0, 5), (W_PASS1, 5), (U_XPASS1, 5), (TERM0, 3),
-    (V_PASS0, 0), (W_PASS1, 1), (U_PASS1, 1), (U_PASS0, 4), (TERM1, 3), (V_PASS0, 3), (V_PASS1, 3),
-    (U_PASS0, 2), (PART, 2), (TERM1, 1), (W_SHARE, 5), (V_CROSS, 0), (TERM1, 0), (U_PASS1, 2), (T_PASS0, 6),
-    (V_PASS1, 0), (U_TURN, 4), (PART, 5), (V_PASS1, 2), (U_PASS0, 1), (W_SHARE, 1), (V_CROSS, 3),
-    (U_XPASS1, 4), (U_PASS1, 0), (T_SHARE, 6), (U_XPASS1, 3), (U_PASS0, 0), (U_XPASS0, 3), (U_XPASS0, 4),
-    (V_PASS0, 5), (V_PASS0, 2), (TERM0, 6), (U_TURN, 1), (TERM1, 6), (U_TURN, 0), (U_TURN, 2), (V_CROSS, 5),
-    (PART, 1), (U_PASS1, 6), (V_CROSS, 2), (U_PASS0, 6), (U_XPASS1, 2), (U_XPASS1, 1), (V_PASS1, 5),
-    (U_XPASS1, 0), (U_TURN, 3), (U_TURN, 5), (U_XPASS0, 2), (U_XPASS0, 0), (V_PASS0, 1), (U_XPASS0, 1),
-    (U_PASS1, 3), (U_TURN, 6), (V_PASS1, 1), (V_END, 3), (V_END, 2), (V_CROSS, 1), (U_END, 4), (U_PASS0, 5),
-    (V_END, 0), (V_END, 4), (U_PASS0, 3), (U_XPASS0, 6), (U_PASS1, 5), (U_END, 2), (U_XPASS1, 6),
-    (U_END, 0), (V_END, 6), (V_END, 5), (U_END, 5), (U_END, 3), (U_END, 1), (V_END, 1), (U_END, 6),
+    (W_OWN, 0), (W_OWN, 5), (W_OWN, 2), (T_OWN, 3), (SLOPE0, 0), (W_OWN, 6), (T_OWN, 1), (S_CROSS, 2),
+    (W_OWN, 4), (SLOPE1, 0), (T_OWN, 6), (W_OTHER, 5), (T_OWN, 4), (W_PASS0, 5), (T_OWN, 2), (W_OTHER, 2),
+    (T_PASS0, 6), (W_OTHER, 0), (W_PASS0, 2), (W_PASS1, 5), (W_OWN, 3), (T_PASS0, 1), (T_PASS0, 3),
+    (T_PASS1, 6), (T_PASS1, 1), (W_PASS1, 2), (S_CROSS, 1), (W_OTHER, 6), (T_OWN, 5), (T_SHARE, 6),
+    (S_CROSS, 0), (T_PASS1, 3), (W_OTHER, 4), (T_PASS0, 2), (W_PASS0, 0), (T_PASS0, 4), (T_OWN, 0),
+    (T_PASS1, 2), (W_OTHER, 3), (W_SHARE, 5), (W_PASS1, 0), (T_SHARE, 3), (W_PASS1, 6), (W_PASS0, 4),
+    (T_PASS1, 4), (S_CROSS, 3), (W_OWN, 1), (PART, 5), (W_SHARE, 2), (T_SHARE, 1), (TERM0, 6), (W_SHARE, 0),
+    (T_SHARE, 4), (TERM0, 3), (W_PASS1, 4), (W_PASS0, 6), (T_PASS0, 5), (V_PASS0, 5), (PART, 2), (TERM0, 4),
+    (W_PASS0, 1), (T_SHARE, 2), (PART, 0), (S_PASS, 0), (U_PASS1, 6), (TERM0, 1), (V_CROSS, 5),
+    (W_OTHER, 1), (T_PASS1, 0), (W_SHARE, 6), (T_PASS1, 5), (W_PASS1, 3), (V_PASS1, 5), (W_SHARE, 4),
+    (W_PASS0, 3), (T_PASS0, 0), (V_PASS0, 2), (TERM0, 2), (U_PASS1, 3), (TERM1, 2), (V_PASS0, 0),
+    (TERM1, 3), (TERM1, 6), (T_SHARE, 0), (T_SHARE, 5), (TERM1, 1), (V_CROSS, 2), (W_SHARE, 3),
+    (V_PASS1, 2), (U_XPASS0, 2), (U_XPASS1, 2), (PART, 6), (V_CROSS, 0), (TERM0, 0), (U_PASS0, 6),
+    (TERM1, 0), (V_PASS1, 0), (V_PASS0, 6), (W_PASS1, 1), (U_PASS1, 1), (U_PASS0, 3), (PART, 3),
+    (U_PASS0, 1), (TERM0, 5), (U_TURN, 6), (PART, 4), (U_XPASS1, 0), (W_SHARE, 1), (U_XPASS0, 0),
+    (TERM1, 4), (V_PASS0, 3), (V_CROSS, 6), (U_TURN, 1), (U_XPASS0, 6), (U_XPASS1, 6), (V_PASS1, 3),
+    (U_PASS1, 4), (TERM1, 5), (V_PASS1, 6), (U_TURN, 3), (V_PASS0, 4), (PART, 1), (U_PASS0, 4),
+    (V_CROSS, 3), (U_XPASS0, 1), (U_PASS0, 5), (V_PASS1, 4), (V_END, 2), (U_XPASS1, 1), (U_PASS1, 5),
+    (U_TURN, 0), (V_CROSS, 4), (U_TURN, 4), (V_PASS0, 1), (U_XPASS0, 3), (U_TURN, 2), (V_END, 3),
+    (U_END, 6), (U_XPASS1, 3), (U_END, 1), (U_TURN, 5), (U_PASS1, 0), (U_PASS0, 0), (U_XPASS1, 4),
+    (U_XPASS0, 4), (V_END, 0), (V_CROSS, 1), (V_PASS1, 1), (U_PASS0, 2), (V_END, 4), (U_XPASS1, 5),
+    (U_PASS1, 2), (V_END, 6), (U_END, 3), (U_XPASS0, 5), (U_END, 2), (U_END, 4), (V_END, 5), (V_END, 1),
+    (U_END, 0), (U_END, 5),
 )
 
 FIRST0 = next(k for name, k in ORDER if name == TERM0)

time: 116 us -> 116 us (level)
  no operation moved by 1% of the time
where the time goes in v5:
time: 116 us; the launch traced here: 115 us
  Pallas kernels  115 us (99%)
    pallas_call x1, Pallas kernels, exchange(): pl.pallas_call(kernel, out_shape=(pltpu.VMEM((CH, RB, HID), F32), pltpu.V...  112 us
    pallas_call x1, Pallas kernels, finish(): pl.pallas_call(finish_kernel, out_shape=(state, state, state, jax.ShapeDt...  2.83 us

profile of v5, /device:TPU:0, one launch (start us, length us, event | category | flops | bytes accessed | tf_op | source)
XLA Modules:
  0.0 115.4 jit_solution(8015507000619787337)
XLA Ops:
  0.6 0.0 copy-start
  0.6 0.0 copy-start.1
  0.7 0.0 copy-start.2
  0.7 111.7 %exchange.1 = (f32[7,32,1280]{2,1,0:T(8,128)S(1)}, bf16[7,512,128]{2,1,0:T(8,128)(2,1)S(1)}) custom-call(bf16[128,3584]{1,0:T(8,128)(2,1)} %tok.1, bf16[1024,1280]{1,0:T(8,128)(2,1)} %pre.1, bf16[1024,1280]{1,0:T(8,128)(2,1)} %cot.1, f32[7,32,1280]{2,1,0:T(8,128)} %bitcast.1), custom_call_target="tpu_custom_call" | custom-call | flops 18790481920 | bytes 12582912 | tf_op jit(solution)/shard_map/exchange/pallas_call | solution.py:481
  112.4 0.0 copy-done
  112.4 0.0 copy-done.1
  112.4 0.0 copy-done.2
  112.4 2.8 %finish.1 = (f32[224,1280]{1,0:T(8,128)}, f32[224,1280]{1,0:T(8,128)}, f32[224,1280]{1,0:T(8,128)}, bf16[128,3584]{1,0:T(8,128)(2,1)}) custom-call(f32[7,32,1280]{2,1,0:T(8,128)S(1)} %get-tuple-element.6.summed, bf16[7,512,128]{2,1,0:T(8,128)(2,1)S(1)} %get-tuple-element.7.turned, f32[224,1280]{1,0:T(8,128)S(1)} %copy-done, f32[224,1280]{1,0:T(8,128)S(1)} %copy-done.1, ...), custom_call_target="tpu_custom_call" | custom-call | tf_op jit(solution)/shard_map/finish/pallas_call | solution.py:579
Async XLA Ops:
  0.6 111.8 %copy-start = (f32[224,1280]{1,0:T(8,128)S(1)}, f32[224,1280]{1,0:T(8,128)}, u32[]{:S(2)}) copy-start(f32[224,1280]{1,0:T(8,128)} %mas.1) | copy-start | bytes 3440644
  0.6 111.8 %copy-start.1 = (f32[224,1280]{1,0:T(8,128)S(1)}, f32[224,1280]{1,0:T(8,128)}, u32[]{:S(2)}) copy-start(f32[224,1280]{1,0:T(8,128)} %first.1) | copy-start | bytes 3440644
  0.7 111.8 %copy-start.2 = (f32[224,1280]{1,0:T(8,128)S(1)}, f32[224,1280]{1,0:T(8,128)}, u32[]{:S(2)}) copy-start(f32[224,1280]{1,0:T(8,128)} %second.1) | copy-start | bytes 3440644

commit v6 on v5

--- a/solution.py
+++ b/solution.py
@@ -82,8 +82,8 @@
 
 
 def kernel(
-    tok, pre, cot, mas, sum_out, ig_out,
-    tg, tc, wg, slope, sx, tb, zf, zn, xf, xs, xf4, xs4, zf1, zs1, ib, yf, yn, xhb, tokv, masv, prev, cotv,
+    tok, pre, cot, mas, first, second, new_mas, new_first, new_second, ig_out,
+    tg, tc, wg, slope, sx, tb, zf, zn, xf, xs, xf4, xs4, zf1, zs1, ib, yf, yn, xhb, tokv, prev, cotv,
     in_sem, st_sem, ts, tr, ws, wr, us, ur, vs, vr, ss, sr,
 ):
     r = lax.axis_index("region")
@@ -104,7 +104,9 @@
     d_y = (device(xl, z, c, xh, yp), device(xl, z, c, xh, ym))
 
     get_tok = pltpu.make_async_copy(tok, tokv, in_sem.at[0])
-    get_mas = pltpu.make_async_copy(mas, masv, in_sem.at[1])
+    get_mas = pltpu.make_async_copy(mas, new_mas, in_sem.at[1])
+    get_first = pltpu.make_async_copy(first, new_first, in_sem.at[2])
+    get_second = pltpu.make_async_copy(second, new_second, in_sem.at[3])
     get_tok.start()
     get_mas.start()
 
@@ -131,6 +133,8 @@
             k, row = place(j * 128 + m * RB)
             half, row = divmod(row, HALF)
             tg[k, y, half, row:row + RB, :] = turned[m * RB:(m + 1) * RB, :]
+    get_first.start()
+    get_second.start()
     pl.semaphore_wait(barrier, 8)
 
     def t_copy(k, slot, i):
@@ -172,7 +176,7 @@
             w_copy(k, 0, i, d_x[0]).wait_recv()
 
     def w_own(k):
-        wg[k, c, z * 2 + xl] = masv[k].astype(BF)
+        wg[k, c, z * 2 + xl] = new_mas[k].astype(BF)
         w_copy(k, z * 2 + xl, 0, d_x[0]).start()
         w_copy(k, z * 2 + xl, 1, d_z[0]).start()
         w_copy(k, z * 2 + xl, 3, d_z[1]).start()
@@ -369,21 +373,28 @@
             to[...] = plus(to, xf.at[n, rows]).astype(BF)
         u_xnear(k, 1 - p, p).start()
 
+    def update(k, summed):
+        pseudo = summed * (RT * REGIONS) ** (-0.5)
+        one = 0.9 * new_first[k] + 0.1 * pseudo
+        two = 0.999 * new_second[k] + 0.001 * pseudo * pseudo
+        new_mas[k] = new_mas[k] - 0.1 * one / (jnp.sqrt(two) + 0.001)
+        new_first[k] = one
+        new_second[k] = two
+
     def u_end(k):
         if k in X_FIRST:
             n = X_FIRST.index(k)
             for p in range(2):
                 for a in range(2):
                     u_near(k, p, a).wait_recv()
-            sum_out[k] = plus(tb.at[k, z, 0, xl], zs1.at[n, 0], zs1.at[n, 1])
+            update(k, plus(tb.at[k, z, 0, xl], zs1.at[n, 0], zs1.at[n, 1]))
         else:
             n = Z_FIRST.index(k)
             for p in range(2):
                 for a in range(2):
                     u_xnear(k, p, a).wait_recv()
-            sum_out[k] = plus(
-                tb.at[k, z, 0, xl], zn.at[n, 0, 0, xl], zn.at[n, 1, 0, xl], xs.at[n, 0], xs.at[n, 1]
-            )
+            near = zn.at[n, 0, 0, xl], zn.at[n, 1, 0, xl]
+            update(k, plus(tb.at[k, z, 0, xl], *near, xs.at[n, 0], xs.at[n, 1]))
         for p in range(2):
             u_far(k, p).wait_send()
             u_xfar(k, p).wait_send()
@@ -466,26 +477,32 @@
         U_END: u_end, PART: part, V_PASS0: v_pass0, V_PASS1: v_pass1,
         V_CROSS: v_cross, V_END: v_end,
     }
-    waited = False
+    waited = ready = False
     for name, k in ORDER:
         if name == W_OWN and not waited:
             get_mas.wait()
             waited = True
+        if name == U_END and not ready:
+            get_first.wait()
+            get_second.wait()
+            ready = True
         work[name](k)
     s_sent()
 
 
-def exchange(tokens, preact, cotangent, master):
+def exchange(tokens, preact, cotangent, master, first, second):
     any_spec = pl.BlockSpec(memory_space=pl.ANY)
     dma = pltpu.SemaphoreType.DMA
     return pl.pallas_call(
         kernel,
         out_shape=(
             pltpu.VMEM((CH, RB, HID), F32),
+            pltpu.VMEM((CH, RB, HID), F32),
+            pltpu.VMEM((CH, RB, HID), F32),
             pltpu.VMEM((CH, CD, TOK), BF),
         ),
-        in_specs=[any_spec] * 4,
-        out_specs=(pl.BlockSpec(memory_space=pltpu.VMEM),) * 2,
+        in_specs=[any_spec] * 6,
+        out_specs=(pl.BlockSpec(memory_space=pltpu.VMEM),) * 4,
         scratch_shapes=[
             pltpu.VMEM((CH, 4, 2, HALF, TOK), BF),
             pltpu.VMEM((CH, 4, HALF, TOK), BF),
@@ -506,10 +523,9 @@
             pltpu.VMEM((CH, 4, CD, TOK), BF),
             pltpu.VMEM((CH, CD, TOK), BF),
             pltpu.VMEM((TOK, D), BF),
-            pltpu.VMEM((CH, RB, HID), F32),
             pltpu.VMEM((2, STAGE, HID), BF),
             pltpu.VMEM((2, STAGE, HID), BF),
-            dma((2,)),
+            dma((4,)),
             dma((2, 2)),
             dma((CH, 5)),
             dma((CH, 5)),
@@ -523,80 +539,48 @@
             dma((6,)),
         ],
         compiler_params=pltpu.CompilerParams(
-            collective_id=0, has_side_effects=True, vmem_limit_bytes=56 * 2**20
+            collective_id=0, has_side_effects=True, vmem_limit_bytes=55 * 2**20
         ),
         cost_estimate=pl.CostEstimate(
             flops=4 * RT * HID * D, bytes_accessed=12 * 2**20, transcendentals=RT * HID
         ),
         name="exchange",
-    )(tokens, preact, cotangent, master)
-
-
-def finish_kernel(
-    summed, turned, mas, first, second, new_mas, new_first, new_second, grad,
-    insv, outv, gradv, in_sem, out_sem, grad_sem,
-):
-    def rows(k):
-        return pl.ds(k * RB, RB)
-
-    def get(k):
-        srcs = (mas.at[rows(k)], first.at[rows(k)], second.at[rows(k)])
-        return [pltpu.make_async_copy(src, insv.at[i, k], in_sem.at[i, k]) for i, src in enumerate(srcs)]
-
-    def put(k):
-        dsts = (new_mas, new_first, new_second)
-        return [
-            pltpu.make_async_copy(outv.at[i, k], dst.at[rows(k)], out_sem.at[i, k]) for i, dst in enumerate(dsts)
-        ]
-
-    put_grad = pltpu.make_async_copy(gradv, grad, grad_sem)
+    )(tokens, preact, cotangent, master, first, second)
+
+
+def finish_kernel(a, b, c, turned, new_a, new_b, new_c, grad, gradv, sems):
+    puts = [pltpu.make_async_copy(src, dst, sems.at[i]) for i, (src, dst) in enumerate(((a, new_a), (b, new_b), (c, new_c)))]
+    for copy in puts:
+        copy.start()
     for j in range(D // 128):
         pieces = []
         for m in range(128 // RB):
             q, row = place(j * 128 + m * RB)
             pieces.append(turned[q, row:row + RB, :])
         gradv[:, j * 128:(j + 1) * 128] = jnp.concatenate(pieces, axis=0).T
-    put_grad.start()
-    for k in range(CH):
-        pseudo = summed[k] * (RT * REGIONS) ** (-0.5)
-        one = 0.9 * first[rows(k), :] + 0.1 * pseudo
-        two = 0.999 * second[rows(k), :] + 0.001 * pseudo * pseudo
-        outv[0, k] = mas[rows(k), :] - 0.1 * one / (jnp.sqrt(two) + 0.001)
-        outv[1, k] = one
-        outv[2, k] = two
-        for copy in put(k):
-            copy.start()
-    put_grad.wait()
-    for k in range(CH):
-        for copy in put(k):
-            copy.wait()
-
-
-def finish(summed, turned, master, first_moment, second_moment):
-    any_spec = pl.BlockSpec(memory_space=pl.ANY)
-    state = jax.ShapeDtypeStruct((OWN, HID), F32)
-    dma = pltpu.SemaphoreType.DMA
+    puts.append(pltpu.make_async_copy(gradv, grad, sems.at[3]))
+    puts[3].start()
+    for copy in puts:
+        copy.wait()
+
+
+def finish(*results):
+    state = jax.ShapeDtypeStruct((CH, RB, HID), F32)
     return pl.pallas_call(
         finish_kernel,
         out_shape=(state, state, state, jax.ShapeDtypeStruct((TOK, D), BF)),
-        in_specs=[pl.BlockSpec(memory_space=pltpu.VMEM)] * 5,
-        out_specs=(any_spec,) * 4,
-        scratch_shapes=[
-            pltpu.VMEM((3, CH, RB, HID), F32),
-            pltpu.VMEM((3, CH, RB, HID), F32),
-            pltpu.VMEM((TOK, D), BF),
-            dma((3, CH)),
-            dma((3, CH)),
-            dma,
-        ],
+        in_specs=[pl.BlockSpec(memory_space=pltpu.VMEM)] * 4,
+        out_specs=(pl.BlockSpec(memory_space=pl.ANY),) * 4,
+        scratch_shapes=[pltpu.VMEM((TOK, D), BF), pltpu.SemaphoreType.DMA((4,))],
         compiler_params=pltpu.CompilerParams(vmem_limit_bytes=16 * 2**20),
         name="finish",
-    )(summed, turned, master, first_moment, second_moment)
+    )(*results)
 
 
 def per_device(tokens, preact, cotangent, master, first_moment, second_moment):
-    summed, turned = exchange(tokens, preact, cotangent, master.reshape(CH, RB, HID))
-    return finish(summed, turned, master, first_moment, second_moment)
+    states = [x.reshape(CH, RB, HID) for x in (master, first_moment, second_moment)]
+    *new, grad = finish(*exchange(tokens, preact, cotangent, *states))
+    return (*[x.reshape(OWN, HID) for x in new], grad)
 
 
 def solution(mesh):

time: 116 us -> 115 us (level)
  no operation moved by 1% of the time
where the time goes in v6:
time: 115 us
  Pallas kernels  114 us (99%)
    pallas_call x1, Pallas kernels, exchange(): pl.pallas_call(kernel, out_shape=(pltpu.VMEM((CH, RB, HID), F32), pltpu.V...  112 us

profile of v6, /device:TPU:0, one launch (start us, length us, event | category | flops | bytes accessed | tf_op | source)
XLA Modules:
  0.0 114.9 jit_solution(4833404364844472835)
XLA Ops:
  0.6 112.0 %exchange.1 = (f32[7,32,1280]{2,1,0:T(8,128)S(1)}, f32[7,32,1280]{2,1,0:T(8,128)S(1)}, f32[7,32,1280]{2,1,0:T(8,128)S(1)}, bf16[7,512,128]{2,1,0:T(8,128)(2,1)S(1)}) custom-call(bf16[128,3584]{1,0:T(8,128)(2,1)} %tok.1, bf16[1024,1280]{1,0:T(8,128)(2,1)} %pre.1, bf16[1024,1280]{1,0:T(8,128)(2,1)} %cot.1, f32[7,32,1280]{2,1,0:T(8,128)} %bitcast.6, ...), custom_call_target="tpu_custom_call" | custom-call | flops 18790481920 | bytes 12582912 | tf_op jit(solution)/shard_map/exchange/pallas_call | solution.py:496
  112.6 2.1 %finish.1 = (f32[7,32,1280]{2,1,0:T(8,128)}, f32[7,32,1280]{2,1,0:T(8,128)}, f32[7,32,1280]{2,1,0:T(8,128)}, bf16[128,3584]{1,0:T(8,128)(2,1)}) custom-call(f32[7,32,1280]{2,1,0:T(8,128)S(1)} %get-tuple-element.12.a, f32[7,32,1280]{2,1,0:T(8,128)S(1)} %get-tuple-element.13.b, f32[7,32,1280]{2,1,0:T(8,128)S(1)} %get-tuple-element.14.c, ...), custom_call_target="tpu_custom_call" | custom-call | tf_op jit(solution)/shard_map/finish/pallas_call | solution.py:569
